TPU v7x, 256 devices: a whole 4x4x8 slice. The times are simulated.
256 devices in a mesh: dp: 8 (over z), table: 32 (over y, x, core).
Axes of the slice: x: 4, y: 4, z: 8, core: 2. Of those that a mesh axis runs over, the one named last changes fastest.
Arguments:
- owners: int32 [512, 1024, 1], P(('dp', 'table')), may hold values from 0 to 31; in each aligned block of 1024 rows (0 to 1023, 1024 to 2047, ..., all dimensions but the last counted through in order) at most 48 rows name the same one
- local_rows: int32 [512, 1024], P(('dp', 'table')), may hold values from 0 to 4095
- lengths: int32 [512], P(('dp', 'table')), may hold values from 256 to 1024, as said below
- destinations: int32 [32, 16], P('table', 'dp'), may hold values from 0 to 15, each once within a row
- table: bfloat16 [131072, 512], P('table'), may hold values from -6 to 6
- gain_in: float32 [512], replicated, may hold values from 0.5 to 1.5
- w_in: bfloat16 [512, 2048], replicated, may hold values from -0.25 to 0.25
- b_in: float32 [2048], replicated, may hold values from -3 to 3
- gain_out: float32 [512], replicated, may hold values from 0.5 to 1.5
- w_out: bfloat16 [512, 512], replicated, may hold values from -0.25 to 0.25
- b_out: float32 [512], replicated, may hold values from -3 to 3
Outputs:
- layer_out: bfloat16 [512, 1024, 512], P(('dp', 'table'))
Inputs may be any that keep to these rules, and one draw needn't show every extreme that they name: `owners`: in the 1024 events of one history no table shard is named more than 48 times; this many is reached in some histories. `lengths`: some history of every draw has exactly 1024 events. `destinations`: each row is a permutation of the 16 slots along dp.
All inputs are finite; a program needn't handle non-finite values.
Results may differ from a plain program's by a relative error of at most 0.0045.
Values may be sent and summed in bfloat16 or wider, within the bound.
A program may use at most 128 MiB of HBM per device.

v0:
```python
import jax
import jax.numpy as jnp
from jax import lax
from jax.sharding import PartitionSpec as P

HEADS = 8


score_scale = 0.125
norm_eps = 1e-05


def layer_norm(values, gain_vec):
    centre = jnp.mean(values, axis=-1, keepdims=True)
    spread = values - centre
    variance = jnp.mean(spread * spread, axis=-1, keepdims=True)
    return spread * lax.rsqrt(variance + norm_eps) * gain_vec


def attend_block(query_block, key_block, value_block, length, first, block_rows, key_count):
    scores = jnp.einsum("qhd,khd->hqk", query_block, key_block, preferred_element_type=jnp.float32)
    query_pos = first + jnp.arange(block_rows)
    key_pos = jnp.arange(key_count)
    allowed = (key_pos[None, :] <= query_pos[:, None]) & (key_pos[None, :] < length)
    weights = jnp.where(allowed[None], jax.nn.silu(scores * score_scale), 0.0).astype(jnp.bfloat16)
    return jnp.einsum("hqk,khd->qhd", weights, value_block, preferred_element_type=jnp.float32)


def hstu_layer(history, length, gain_in, w_in, b_in, gain_out, w_out, b_out):
    events = history.shape[0]
    model_width = history.shape[1]
    head_size = model_width // HEADS
    hist_float = history.astype(jnp.float32)
    normed = layer_norm(hist_float, gain_in).astype(jnp.bfloat16)
    active = jax.nn.silu(jnp.dot(normed, w_in, preferred_element_type=jnp.float32) + b_in)
    gate_part = active[:, :model_width]
    value_part = (
        active[:, model_width : 2 * model_width]
        .astype(jnp.bfloat16)
        .reshape(events, HEADS, head_size)
    )
    query_part = (
        active[:, 2 * model_width : 3 * model_width]
        .astype(jnp.bfloat16)
        .reshape(events, HEADS, head_size)
    )
    key_part = active[:, 3 * model_width :].astype(jnp.bfloat16).reshape(events, HEADS, head_size)
    block_rows = min(512, events)
    position = jnp.arange(events)
    pieces = []
    for block_id in range(events // block_rows):
        first = block_id * block_rows
        query_block = query_part[first : first + block_rows]
        piece = attend_block(query_block, key_part, value_part, length, first, block_rows, events)
        pieces.append(piece)
    attended = jnp.concatenate(pieces, 0).reshape(events, model_width)
    gated_rows = (layer_norm(attended, gain_out) * gate_part).astype(jnp.bfloat16)
    update = jnp.dot(gated_rows, w_out, preferred_element_type=jnp.float32) + b_out
    return jnp.where(position[:, None] < length, hist_float + update, 0.0).astype(jnp.bfloat16)


def look_up(owner_ids, row_ids, counts, table_shard):
    seqs_here, events = row_ids.shape
    shards = lax.axis_size("table")
    capacity = seqs_here * (3 * events // (2 * shards))
    flat_count = seqs_here * events
    present = (jnp.arange(events)[None, :] < counts[:, None]).reshape(flat_count)
    owner_flat = owner_ids.reshape(flat_count)
    row_flat = row_ids.reshape(flat_count)
    matches = (owner_flat[:, None] == jnp.arange(shards, dtype=jnp.int32)[None, :]) & present[
        :, None
    ]
    rank_all = jnp.cumsum(matches.astype(jnp.int32), axis=0) - 1
    rank_own = jnp.sum(jnp.where(matches, rank_all, 0), axis=1)
    slot_index = jnp.where(present, owner_flat * capacity + rank_own, shards * capacity)
    request = jnp.zeros((shards * capacity,), jnp.int32).at[slot_index].set(row_flat, mode="drop")
    request = request.reshape(shards, capacity)
    asked_rows = lax.all_to_all(request, "table", split_axis=0, concat_axis=0, tiled=True)
    found_rows = jnp.take(table_shard, asked_rows.reshape(-1), axis=0)
    found_rows = found_rows.reshape(asked_rows.shape + (table_shard.shape[1],))
    answered = lax.all_to_all(found_rows, "table", split_axis=0, concat_axis=0, tiled=True)
    flat_rows = answered.reshape(shards * capacity, table_shard.shape[1])
    picked = jnp.take(flat_rows, jnp.minimum(slot_index, shards * capacity - 1), axis=0)
    picked = jnp.where(present[:, None], picked, 0)
    return picked.reshape(seqs_here, events, table_shard.shape[1])


def on_device(
    owners, local_rows, lengths, destinations, table, gain_in, w_in, b_in, gain_out, w_out, b_out
):
    seqs_here, events = local_rows.shape
    ranks_dp = lax.axis_size("dp")
    position_dp = lax.axis_index("dp")
    every_dest, every_len = (
        lax.all_gather(destinations, "dp", axis=1, tiled=True),
        lax.all_gather(lengths, "dp", axis=0, tiled=True),
    )
    my_slots = position_dp * seqs_here + jnp.arange(seqs_here, dtype=jnp.int32)
    arrivals = (every_dest[0][:, None] == my_slots[None, :]).astype(jnp.int32)
    column_ids = jnp.arange(ranks_dp * seqs_here, dtype=jnp.int32)
    sender = jnp.sum(arrivals * (column_ids // seqs_here)[:, None], axis=0)
    new_lengths = jnp.sum(arrivals * every_len[:, None], axis=0)
    going_to = destinations[0]
    to_device = going_to // seqs_here
    to_slot = going_to % seqs_here
    slot_ids = jnp.arange(seqs_here, dtype=jnp.int32)
    owner_here = owners[:, :, 0]
    owner_out = (
        jnp.zeros((ranks_dp, seqs_here, events), jnp.int32).at[to_device, to_slot].set(owner_here)
    )
    row_out = (
        jnp.zeros((ranks_dp, seqs_here, events), jnp.int32).at[to_device, to_slot].set(local_rows)
    )
    owner_in, row_in = (
        lax.all_to_all(owner_out, "dp", split_axis=0, concat_axis=0, tiled=True),
        lax.all_to_all(row_out, "dp", split_axis=0, concat_axis=0, tiled=True),
    )
    histories = look_up(owner_in[sender, slot_ids], row_in[sender, slot_ids], new_lengths, table)

    def per_history(history_pair):
        return hstu_layer(
            history_pair[0], history_pair[1], gain_in, w_in, b_in, gain_out, w_out, b_out
        )

    return lax.map(per_history, (histories, new_lengths))


def solution(mesh):
    placed = (
        P(("dp", "table"), None, None),
        P(("dp", "table"), None),
        P(("dp", "table")),
        P("table", "dp"),
        P("table", None),
        P(),
        P(),
        P(),
        P(),
        P(),
        P(),
    )
    return jax.shard_map(
        on_device,
        mesh=mesh,
        in_specs=placed,
        out_specs=P(("dp", "table"), None, None),
        check_vma=False,
    )
```

profile of v0, /device:TPU:1, one launch (start us, length us, event | category | flops | bytes accessed | tf_op | source)
XLA Modules:
  0.0 234.5 jit_solution(12736550976040518492)
XLA Ops:
  2.0 2.2 scatter_fusion
  4.2 9.0 %all-to-all-start = ((s32[8,2,1024]{2,1,0:T(2,128)}), s32[8,2,1024]{2,1,0:T(2,128)S(1)}, u32[]{:S(2)}, u32[]{:S(2)}) async-start(s32[8,2,1024]{2,1,0:T(2,128)} %scatter_fusion), calls=%async_computation | async-start | bytes 131072 | tf_op jit(solution)/shard_map/all_to_all | solution.py:115
  16.9 10.8 %all-reduce.2 = (s32[16]{0:T(128)S(1)}, s32[16]{0:T(128)S(1)}) all-reduce(s32[16]{0:T(128)S(1)} %bitcast_dynamic-update-slice_fusion, s32[16]{0:T(128)S(1)} %dynamic-update-slice.1), channel_id=1, replica_groups=mesh['dp'=8,'table'=32] {'dp'}, use_global_device_ids=true, to_apply=%add | all-reduce | flops 32 | bytes 256
  28.8 2.1 scatter_fusion.1
  31.0 3.4 %all-to-all-start.1 = ((s32[8,2,1024]{2,1,0:T(2,128)}), s32[8,2,1024]{2,1,0:T(2,128)S(1)}, u32[]{:S(2)}, u32[]{:S(2)}) async-start(s32[8,2,1024]{2,1,0:T(2,128)} %scatter_fusion.1), calls=%async_computation.1 | async-start | bytes 131072 | tf_op jit(solution)/shard_map/all_to_all | solution.py:116
  35.0 9.1 %reduce-window.6 = s32[32,16,128]{2,1,0:T(8,128)S(1)} reduce-window(s32[32,16,128]{2,1,0:T(8,128)S(1)} %fusion.39, s32[]{:T(128)} %copy.85), window={size=1x1x128 pad=0_0x0_0x127_0}, to_apply=%region_3.4 | reduce-window | flops 8323072 | bytes 524292 | tf_op jit(solution)/shard_map/reduce-window
  45.8 8.1 %scatter_custom_fusion.2 = s32[3072]{0:T(1024)S(1)} fusion(s32[2048]{0:T(1024)S(1)} %bitcast.203, s32[2048]{0:T(1024)S(1)} %bitcast.204, s32[]{:T(128)} %copy.85), kind=kCustom, calls=%fused_computation.81 | custom fusion | bytes 12292 | tf_op jit(solution)/shard_map/scatter | solution.py:76
  53.9 18.2 %all_to_all.24 = s32[32,1,96]{2,1,0:T(1,128)S(1)} all-to-all(s32[32,1,96]{2,1,0:T(1,128)S(1)} %all_to_all.17), channel_id=1, replica_groups=mesh['dp'=8,'table'=32] {'table'}, dimensions={0} | all-to-all | bytes 24576 | tf_op jit(solution)/shard_map/all_to_all | solution.py:78
  73.5 13.9 %gather_fusion.2 = bf16[3072,512]{1,0:T(8,128)(2,1)S(1)} fusion(bf16[4096,512]{1,0:T(8,128)(2,1)} %param.17, s32[3072]{0:T(1024)S(1)} %broadcast_clamp_fusion), kind=kCustom, calls=%fused_computation.2 | custom fusion | bytes 6303744 | tf_op jit(solution)/shard_map/jit(_take)/gather | solution.py:79
  87.4 2.0 broadcast_select_fusion
  89.4 4.4 %all-to-all-start.3 = ((bf16[32,96,512]{2,1,0:T(8,128)(2,1)}), bf16[32,96,512]{2,1,0:T(8,128)(2,1)S(1)}, u32[]{:S(2)}, u32[]{:S(2)}) async-start(bf16[32,96,512]{2,1,0:T(8,128)(2,1)} %broadcast_select_fusion), calls=%async_computation.3 | async-start | bytes 6291456 | tf_op jit(solution)/shard_map/all_to_all | solution.py:81
  93.8 39.2 %all-to-all-done.3 = bf16[32,96,512]{2,1,0:T(8,128)(2,1)S(1)} async-done(((bf16[32,96,512]{2,1,0:T(8,128)(2,1)}), bf16[32,96,512]{2,1,0:T(8,128)(2,1)S(1)}, u32[]{:S(2)}, u32[]{:S(2)}) %all-to-all-start.3) | async-done | bytes 3145760 | tf_op jit(solution)/shard_map/all_to_all | solution.py:81
  133.0 9.2 %gather_fusion.3 = bf16[2048,512]{1,0:T(8,128)(2,1)} fusion(bf16[3072,512]{1,0:T(8,128)(2,1)S(1)} %bitcast.181, s32[2048]{0:T(1024)S(1)} %broadcast_clamp_fusion.1), kind=kCustom, calls=%fused_computation.3 | custom fusion | bytes 4202496 | tf_op jit(solution)/shard_map/jit(_take)/gather | solution.py:83
  142.2 2.9 %select_select_fusion = bf16[2,1024,512]{2,1,0:T(8,128)(2,1)S(1)} fusion(bf16[2,1024,512]{2,1,0:T(8,128)(2,1)} %bitcast.189, pred[2,1024]{1,0:T(4,128)(4,1)S(1)} %get-tuple-element.94, pred[2,1024]{1,0:T(4,128)(4,1)S(1)} %iota_compare_fusion.5), kind=kLoop, calls=%fused_computation.57 | loop fusion | flops 2097152 | bytes 4198400 | tf_op jit(solution)/shard_map/jit(_where)/select_n | solution.py:84
  145.1 89.4 %while.11 = (s32[]{:T(128)}, bf16[2,1024,512]{2,1,0:T(8,128)(2,1)}, s32[2]{0:T(128)S(1)}, bf16[2,1024,512]{2,1,0:T(8,128)(2,1)S(1)}, f32[512]{0:T(512)S(1)}, /*i...) while((s32[]{:T(128)}, bf16[2,1024,512]{2,1,0:T(8,128)(2,1)}, ...), condition=%wide.region_13.14_spmd.clone, body=%wide.region_8.13_spmd.sunk.clone | while | flops 4919397888 | bytes 103380752 | solution.py:125
  147.7 5.8 %fusion.108 = (bf16[1024,2048]{1,0:T(8,128)(2,1)S(1)}, f32[1024,2048]{1,0:T(8,128)}) fusion(f32[2048]{0:T(1024)S(1)} %get-tuple-element.235, bf16[512,2048]{1,0:T(8,128)(2,1)S(1)} %copy-done.4, f32[512]{0:T(512)S(1)} %get-tuple-element.233, f32[1024]{0:T(1024)S(1)} %add_rsqrt_fusion.6, f32[1024]{0:T(1024)S(1)} %broadcast_multiply_fusion.6, ...), kind=kOutput, calls=%fused_computation.116.clone.1.clone | convolution fusion | flops 2162688000 | bytes 15747076 | tf_op jit(solution)/shard_map/while/body/eval_jaxpr/dot_general | solution.py:35
  162.2 8.7 %fusion.113 = f32[512,8,64]{0,2,1:T(8,128)S(1)} fusion(bf16[1024,8,64]{0,2,1:T(8,128)(2,1)S(1)} %bitcast.182, bf16[512,8,64]{0,2,1:T(8,128)(2,1)} %bitcast.186, bf16[1024,8,64]{0,2,1:T(8,128)(2,1)} %bitcast.184, pred[512,1024]{1,0:T(8,128)(4,1)S(1)} %get-tuple-element.195), kind=kOutput, calls=%fused_computation.32.clone.1.clone | convolution fusion | flops 1103101952 | bytes 4194304 | tf_op jit(solution)/shard_map/while/body/eval_jaxpr/hqk,khd->qhd/dot_general | solution.py:26
  171.9 8.8 %fusion.112 = f32[512,8,64]{0,2,1:T(8,128)S(1)} fusion(bf16[1024,8,64]{0,2,1:T(8,128)(2,1)S(1)} %bitcast.183, bf16[512,8,64]{0,2,1:T(8,128)(2,1)} %bitcast.187, bf16[1024,8,64]{0,2,1:T(8,128)(2,1)} %bitcast.185, pred[512,1024]{1,0:T(8,128)(4,1)} %get-tuple-element.193), kind=kOutput, calls=%fused_computation.31.clone.1.clone | convolution fusion | flops 1103101952 | bytes 4194304 | tf_op jit(solution)/shard_map/while/body/eval_jaxpr/hqk,khd->qhd/dot_general | solution.py:26
  183.4 1.9 copy.68
  185.3 4.6 %fusion.115 = bf16[2,1024,512]{2,1,0:T(8,128)(2,1)} fusion(bf16[2,1024,512]{2,1,0:T(8,128)(2,1)} %get-tuple-element.220, s32[]{:T(128)} %get-tuple-element.219, bf16[512,512]{1,0:T(8,128)(2,1)} %get-tuple-element.237, f32[1024,2048]{1,0:T(8,128)} %get-tuple-element.188, f32[1024,512]{1,0:T(8,128)} %copy.68, f32[512]{0:T(512)S(1)} %get-tuple-element.238, ...), kind=kOutput, calls=%fused_computation.34.clone.1.clone | convolution fusion | flops 542113792 | bytes 6829568 | tf_op jit(solution)/shard_map/while/body/eval_jaxpr/dot_general | solution.py:58
  192.3 5.8 %fusion.108 = (bf16[1024,2048]{1,0:T(8,128)(2,1)S(1)}, f32[1024,2048]{1,0:T(8,128)}) fusion(f32[2048]{0:T(1024)S(1)} %get-tuple-element.235, bf16[512,2048]{1,0:T(8,128)(2,1)S(1)} %copy-done.4, f32[512]{0:T(512)S(1)} %get-tuple-element.233, f32[1024]{0:T(1024)S(1)} %add_rsqrt_fusion.6, f32[1024]{0:T(1024)S(1)} %broadcast_multiply_fusion.6, ...), kind=kOutput, calls=%fused_computation.116.clone.1.clone | convolution fusion | flops 2162688000 | bytes 15747076 | tf_op jit(solution)/shard_map/while/body/eval_jaxpr/dot_general | solution.py:35
  206.8 8.7 %fusion.113 = f32[512,8,64]{0,2,1:T(8,128)S(1)} fusion(bf16[1024,8,64]{0,2,1:T(8,128)(2,1)S(1)} %bitcast.182, bf16[512,8,64]{0,2,1:T(8,128)(2,1)} %bitcast.186, bf16[1024,8,64]{0,2,1:T(8,128)(2,1)} %bitcast.184, pred[512,1024]{1,0:T(8,128)(4,1)S(1)} %get-tuple-element.195), kind=kOutput, calls=%fused_computation.32.clone.1.clone | convolution fusion | flops 1103101952 | bytes 4194304 | tf_op jit(solution)/shard_map/while/body/eval_jaxpr/hqk,khd->qhd/dot_general | solution.py:26
  216.5 8.8 %fusion.112 = f32[512,8,64]{0,2,1:T(8,128)S(1)} fusion(bf16[1024,8,64]{0,2,1:T(8,128)(2,1)S(1)} %bitcast.183, bf16[512,8,64]{0,2,1:T(8,128)(2,1)} %bitcast.187, bf16[1024,8,64]{0,2,1:T(8,128)(2,1)} %bitcast.185, pred[512,1024]{1,0:T(8,128)(4,1)} %get-tuple-element.193), kind=kOutput, calls=%fused_computation.31.clone.1.clone | convolution fusion | flops 1103101952 | bytes 4194304 | tf_op jit(solution)/shard_map/while/body/eval_jaxpr/hqk,khd->qhd/dot_general | solution.py:26
  229.8 4.6 %fusion.115 = bf16[2,1024,512]{2,1,0:T(8,128)(2,1)} fusion(bf16[2,1024,512]{2,1,0:T(8,128)(2,1)} %get-tuple-element.220, s32[]{:T(128)} %get-tuple-element.219, bf16[512,512]{1,0:T(8,128)(2,1)} %get-tuple-element.237, f32[1024,2048]{1,0:T(8,128)} %get-tuple-element.188, f32[1024,512]{1,0:T(8,128)} %copy.68, f32[512]{0:T(512)S(1)} %get-tuple-element.238, ...), kind=kOutput, calls=%fused_computation.34.clone.1.clone | convolution fusion | flops 542113792 | bytes 6829568 | tf_op jit(solution)/shard_map/while/body/eval_jaxpr/dot_general | solution.py:58
  (113 shorter events, 41.2 us)
Async XLA Ops:
  4.2 26.8 %all-to-all-start = ((s32[8,2,1024]{2,1,0:T(2,128)}), s32[8,2,1024]{2,1,0:T(2,128)S(1)}, u32[]{:S(2)}, u32[]{:S(2)}) async-start(s32[8,2,1024]{2,1,0:T(2,128)} %scatter_fusion), calls=%async_computation | async-start | bytes 131072 | tf_op jit(solution)/shard_map/all_to_all | solution.py:115
  31.0 14.1 %all-to-all-start.1 = ((s32[8,2,1024]{2,1,0:T(2,128)}), s32[8,2,1024]{2,1,0:T(2,128)S(1)}, u32[]{:S(2)}, u32[]{:S(2)}) async-start(s32[8,2,1024]{2,1,0:T(2,128)} %scatter_fusion.1), calls=%async_computation.1 | async-start | bytes 131072 | tf_op jit(solution)/shard_map/all_to_all | solution.py:116
  89.4 43.6 %all-to-all-start.3 = ((bf16[32,96,512]{2,1,0:T(8,128)(2,1)}), bf16[32,96,512]{2,1,0:T(8,128)(2,1)S(1)}, u32[]{:S(2)}, u32[]{:S(2)}) async-start(bf16[32,96,512]{2,1,0:T(8,128)(2,1)} %broadcast_select_fusion), calls=%async_computation.3 | async-start | bytes 6291456 | tf_op jit(solution)/shard_map/all_to_all | solution.py:81
  142.2 2.9 %copy-start.5 = (f32[2048]{0:T(1024)S(1)}, f32[2048]{0:T(1024)}, u32[]{:S(2)}) copy-start(f32[2048]{0:T(1024)} %param.20) | copy-start | bytes 24580
  142.2 2.9 %copy-start.6 = (f32[512]{0:T(512)S(1)}, f32[512]{0:T(512)}, u32[]{:S(2)}) copy-start(f32[512]{0:T(512)} %param.18) | copy-start | bytes 6148
  142.2 2.9 %copy-start.7 = (f32[512]{0:T(512)S(1)}, f32[512]{0:T(512)}, u32[]{:S(2)}) copy-start(f32[512]{0:T(512)} %param.21) | copy-start | bytes 6148
  142.2 2.9 %copy-start.8 = (f32[512]{0:T(512)S(1)}, f32[512]{0:T(512)}, u32[]{:S(2)}) copy-start(f32[512]{0:T(512)} %param.23) | copy-start | bytes 6148
  145.3 8.2 %copy-start.1 = (bf16[2,1024,512]{2,1,0:T(8,128)(2,1)}, bf16[2,1024,512]{2,1,0:T(8,128)(2,1)S(1)}, u32[]{:S(2)}) copy-start(bf16[2,1024,512]{2,1,0:T(8,128)(2,1)S(1)} %get-tuple-element.232) | copy-start | bytes 6291460 | tf_op jit(solution)/shard_map/while
  145.3 2.4 %copy-start.4 = (bf16[512,2048]{1,0:T(8,128)(2,1)S(1)}, bf16[512,2048]{1,0:T(8,128)(2,1)}, u32[]{:S(2)}) copy-start(bf16[512,2048]{1,0:T(8,128)(2,1)} %get-tuple-element.234) | copy-start | bytes 6291460 | tf_op jit(solution)/shard_map/while
  153.5 2.0 copy-start.3
  180.7 1.1 copy-start
  185.3 4.6 %copy-start.2 = (bf16[2,1024,512]{2,1,0:T(8,128)(2,1)S(1)}, bf16[2,1024,512]{2,1,0:T(8,128)(2,1)}, u32[]{:S(2)}) copy-start(bf16[2,1024,512]{2,1,0:T(8,128)(2,1)} %copy-done.1) | copy-start | bytes 6291460 | tf_op jit(solution)/shard_map/while
  189.9 8.2 %copy-start.1 = (bf16[2,1024,512]{2,1,0:T(8,128)(2,1)}, bf16[2,1024,512]{2,1,0:T(8,128)(2,1)S(1)}, u32[]{:S(2)}) copy-start(bf16[2,1024,512]{2,1,0:T(8,128)(2,1)S(1)} %get-tuple-element.232) | copy-start | bytes 6291460 | tf_op jit(solution)/shard_map/while
  189.9 2.3 %copy-start.4 = (bf16[512,2048]{1,0:T(8,128)(2,1)S(1)}, bf16[512,2048]{1,0:T(8,128)(2,1)}, u32[]{:S(2)}) copy-start(bf16[512,2048]{1,0:T(8,128)(2,1)} %get-tuple-element.234) | copy-start | bytes 6291460 | tf_op jit(solution)/shard_map/while
  198.1 2.0 copy-start.3
  225.3 1.1 copy-start
  229.8 4.6 %copy-start.2 = (bf16[2,1024,512]{2,1,0:T(8,128)(2,1)S(1)}, bf16[2,1024,512]{2,1,0:T(8,128)(2,1)}, u32[]{:S(2)}) copy-start(bf16[2,1024,512]{2,1,0:T(8,128)(2,1)} %copy-done.1) | copy-start | bytes 6291460 | tf_op jit(solution)/shard_map/while
where the time goes:
time: 237 us; the launch traced here: 234 us
  local copies, waits for them, and re-layouts  67.4 us (28%)
  matrix products  55.7 us (24%)
  waiting for transfers between devices  39.2 us (17%)
  blocking collectives  29 us (12%)
  other arithmetic  25 us (11%)
  starting transfers between devices  16.7 us (7%)
    all_to_all x1, waiting for transfers between devices, look_up(): lax.all_to_all(found_rows, 'table', split_axis=0, concat_axis=0, tiled=True)  39.2 us
    dot_general x4, matrix products, attend_block(): jnp.einsum('hqk,khd->qhd', weights, value_block, preferred_element_type=j...  34.8 us
    all_to_all x1, blocking collectives, look_up(): lax.all_to_all(request, 'table', split_axis=0, concat_axis=0, tiled=True)  18.2 us
    gather x1, local copies, waits for them, and re-layouts, look_up(): found_rows = jnp.take(table_shard, asked_rows.reshape(-1), axis=0)  13.9 us
    dot_general x2, matrix products, hstu_layer(): jnp.dot(normed, w_in, preferred_element_type=jnp.float32) + b_in  11.6 us
    unnamed x1, blocking collectives  10.8 us
    dot_general x2, matrix products, hstu_layer(): jnp.dot(gated_rows, w_out, preferred_element_type=jnp.float32) + b_out  9.28 us
    another operation x2, other arithmetic  9.27 us
  transfers between devices with their start and end apart: 3, of which 1 were waited for; matrix products, arithmetic and copies ran while one was open for 7% of the time, Pallas kernels for 0%

commit v1 on v0

v1 whole, which is shorter than its diff:
```python
import functools
import jax
import jax.numpy as jnp
from jax import lax
from jax.experimental import pallas as pl
from jax.experimental.pallas import tpu as pltpu
from jax.sharding import PartitionSpec as P

HEADS = 8
EPS = 1e-05
BLK = 256
BF = jnp.bfloat16
F32 = jnp.float32


def silu_half(u):
    return u + u * jnp.tanh(u)


def norm_rows(values, gain):
    centre = jnp.mean(values, axis=-1, keepdims=True)
    spread = values - centre
    variance = jnp.mean(spread * spread, axis=-1, keepdims=True)
    return spread * lax.rsqrt(variance + EPS) * gain


def layer_kernel(slot_ref, rows_ref, gain_in_ref, w_in_ref, b_in_ref, gain_out_ref, w_out_ref, b_out_ref,
                 out_ref, hist, gate, q, k, v0, v1, att):
    events, width = hist.shape
    slots = rows_ref.shape[0]
    lanes = lax.broadcasted_iota(jnp.int32, (128, 128), 1)
    subs = lax.broadcasted_iota(jnp.int32, (128, 128), 0)
    eye = lanes == subs
    half = lax.broadcasted_iota(jnp.int32, (BLK, 128), 1) < 64

    def project(c, carry):
        cols = []
        for i in range(BLK // 128):
            line = slot_ref[pl.ds(c * (BLK // 128) + i, 1), :]
            spread = jnp.where(eye, jnp.broadcast_to(line, (128, 128)), 0)
            cols.append(jnp.sum(spread, axis=1, keepdims=True))
        col = jnp.concatenate(cols, axis=0)
        here = (col >= 0).astype(F32)
        pick = (col == lax.broadcasted_iota(jnp.int32, (BLK, slots), 1)).astype(F32).astype(BF)
        rows = jnp.dot(pick, rows_ref[...], preferred_element_type=F32)
        at = pl.ds(pl.multiple_of(c * BLK, BLK), BLK)
        hist[at, :] = rows.astype(BF)
        normed = norm_rows(rows, gain_in_ref[...]).astype(BF)
        for part in range(4):
            cs = slice(part * width, (part + 1) * width)
            pre = jnp.dot(normed, w_in_ref[:, cs], preferred_element_type=F32) + b_in_ref[:, cs]
            act = silu_half(0.5 * pre)
            if part == 0:
                gate[at, :] = act
            elif part == 1:
                act = act * here
                for p in range(4):
                    piece = act[:, p * 128:(p + 1) * 128]
                    v0[p, at, :] = jnp.where(half, piece, 0.0).astype(BF)
                    v1[p, at, :] = jnp.where(half, 0.0, piece).astype(BF)
            else:
                target = q if part == 2 else k
                act = act.astype(BF)
                for p in range(4):
                    target[p, at, :] = act[:, p * 128:(p + 1) * 128]
        return carry

    lax.fori_loop(0, events // BLK, project, 0)

    tri = lax.broadcasted_iota(jnp.int32, (BLK, BLK), 0) >= lax.broadcasted_iota(jnp.int32, (BLK, BLK), 1)

    def attend(p, carry):
        for i in range(events // BLK):
            at = slice(i * BLK, (i + 1) * BLK)
            qb = q[p, at, :] * jnp.bfloat16(0.0625)
            total = None
            for h, v in ((0, v0), (1, v1)):
                qh = jnp.where(half == (h == 0), qb.astype(F32), 0.0).astype(BF)
                for j in range(i + 1):
                    ks = slice(j * BLK, (j + 1) * BLK)
                    s = lax.dot_general(qh, k[p, ks, :], (((1,), (1,)), ((), ())), preferred_element_type=F32)
                    w = silu_half(s)
                    if j == i:
                        w = jnp.where(tri, w, 0.0)
                    o = jnp.dot(w.astype(BF), v[p, ks, :], preferred_element_type=F32)
                    total = o if total is None else total + o
            att[p, at, :] = total
        return carry

    lax.fori_loop(0, 4, attend, 0)

    def finish(c, carry):
        cols = []
        for i in range(BLK // 128):
            line = slot_ref[pl.ds(c * (BLK // 128) + i, 1), :]
            spread = jnp.where(eye, jnp.broadcast_to(line, (128, 128)), 0)
            cols.append(jnp.sum(spread, axis=1, keepdims=True))
        here = jnp.concatenate(cols, axis=0) >= 0
        at = pl.ds(pl.multiple_of(c * BLK, BLK), BLK)
        full = jnp.concatenate([att[p, at, :] for p in range(4)], axis=1)
        gated = (norm_rows(full, gain_out_ref[...]) * gate[at, :]).astype(BF)
        update = jnp.dot(gated, w_out_ref[...], preferred_element_type=F32) + b_out_ref[...]
        out_ref[0, at, :] = jnp.where(here, hist[at, :].astype(F32) + update, 0.0).astype(BF)
        return carry

    lax.fori_loop(0, events // BLK, finish, 0)


def layer_call(s, slot, rows, gain_in, w_in, b_in, gain_out, w_out, b_out, before):
    events = slot.shape[0] * 128
    width = rows.shape[1]
    vm = pl.BlockSpec(memory_space=pltpu.VMEM)
    ins = [slot, rows, gain_in[None], w_in, b_in[None], gain_out[None], w_out, b_out[None]]
    specs = [vm] * len(ins)
    kernel = layer_kernel
    aliases = {}
    if before is not None:
        ins.append(before)
        specs.append(pl.BlockSpec(memory_space=pl.ANY))
        aliases = {len(ins) - 1: 0}

        def kernel(*refs):
            layer_kernel(*refs[:8], *refs[9:])
    return pl.pallas_call(
        kernel,
        grid=(1,),
        in_specs=specs,
        out_specs=pl.BlockSpec((1, events, width), lambda i: (s, 0, 0)),
        out_shape=jax.ShapeDtypeStruct((2, events, width), BF),
        scratch_shapes=[
            pltpu.VMEM((events, width), BF),
            pltpu.VMEM((events, width), F32),
            pltpu.VMEM((4, events, 128), BF),
            pltpu.VMEM((4, events, 128), BF),
            pltpu.VMEM((4, events, 128), BF),
            pltpu.VMEM((4, events, 128), BF),
            pltpu.VMEM((4, events, 128), F32),
        ],
        input_output_aliases=aliases,
        compiler_params=pltpu.CompilerParams(vmem_limit_bytes=40 << 20),
        cost_estimate=pl.CostEstimate(flops=8 * 10**9, bytes_accessed=8 << 20, transcendentals=8 << 20),
        name="layer",
    )(*ins)
MESH = pl.DeviceIdType.MESH
SLOTS = 48
INT = jnp.int32


def route_kernel(seqs, n_dp, n_table, owners_ref, rows_ref, lengths_ref, dest_ref, asked_ref, slot_ref,
                 mine, every, req, send_z, recv_z, send_t, recv_t):
    me_dp, me_t = lax.axis_index("dp"), lax.axis_index("table")
    events = owners_ref.shape[1]
    lines = events // 128
    barrier = pltpu.get_barrier_semaphore()
    for i in range(1, n_dp):
        pl.semaphore_signal(barrier, inc=1, device_id={"dp": lax.rem(me_dp + i, n_dp)}, device_id_type=MESH)

    @pl.loop(1, n_table)
    def _(i):
        pl.semaphore_signal(barrier, inc=1, device_id={"table": lax.rem(me_t + i, n_table)}, device_id_type=MESH)

    lane = lax.broadcasted_iota(INT, (1, 128), 1)
    for s in range(seqs):
        for r in range(lines):
            cs = slice(r * 128, (r + 1) * 128)
            packed = owners_ref[s:s + 1, cs] * 4096 + rows_ref[s:s + 1, cs]
            mine[s * lines + r:s * lines + r + 1, :] = jnp.where(lane + r * 128 < lengths_ref[s], packed, -1)
    for j in range(8):
        mine[seqs * lines + j:seqs * lines + j + 1, :] = jnp.zeros((1, 128), INT) + dest_ref[0, min(j, seqs - 1)]
    every[me_dp] = mine[...]
    pl.semaphore_wait(barrier, n_dp - 1 + n_table - 1)

    copies = []
    for i in range(1, n_dp):
        copy = pltpu.make_async_remote_copy(
            src_ref=mine, dst_ref=every.at[me_dp], send_sem=send_z.at[i], recv_sem=recv_z.at[me_dp],
            device_id={"dp": lax.rem(me_dp + i, n_dp)}, device_id_type=MESH)
        copy.start()
        copies.append(copy)
    for i in range(1, n_dp):
        pltpu.make_async_remote_copy(
            src_ref=mine, dst_ref=every.at[lax.rem(me_dp + i, n_dp)], send_sem=send_z.at[i],
            recv_sem=recv_z.at[lax.rem(me_dp + i, n_dp)],
            device_id={"dp": lax.rem(me_dp + i, n_dp)}, device_id_type=MESH).wait_recv()

    shard = lax.broadcasted_iota(INT, (n_table, 128), 0)
    place = lax.broadcasted_iota(INT, (128, 128), 0)
    upper = (place <= lax.broadcasted_iota(INT, (128, 128), 1)).astype(F32).astype(BF)
    request = jnp.zeros((2 * n_table, 128), F32)
    for s in range(seqs):
        refs = jnp.zeros((lines, 128), INT)
        for d in range(n_dp):
            for j in range(seqs):
                went = every[d, seqs * lines + j:seqs * lines + j + 1, :]
                refs += jnp.where(went == me_dp * seqs + s, every[d, j * lines:(j + 1) * lines, :], 0)
        owner, row = refs >> 12, refs & 4095
        named = [(jnp.broadcast_to(owner[r:r + 1, :], (n_table, 128)) == shard) for r in range(lines)]
        before = jnp.zeros((n_table, 1), F32)
        for r in range(lines):
            hot = named[r].astype(F32)
            upto = jnp.dot(hot.astype(BF), upper, preferred_element_type=F32) + before
            before += jnp.sum(hot, axis=1, keepdims=True)
            rank = jnp.sum(jnp.where(named[r], upto - 1.0, 0.0), axis=0, keepdims=True)
            slot = jnp.sum(jnp.where(named[r], upto + (shard * SLOTS).astype(F32), 0.0), axis=0, keepdims=True)
            slot_ref[s, r:r + 1, :] = slot.astype(INT) - 1
            high = jnp.broadcast_to(row[r:r + 1, :] >> 6, (n_table, 128)).astype(F32)
            low = jnp.broadcast_to(row[r:r + 1, :] & 63, (n_table, 128)).astype(F32)
            left = jnp.concatenate([jnp.where(named[r], high, 0.0), jnp.where(named[r], low, 0.0)], axis=0)
            right = jnp.broadcast_to(rank.astype(INT) + s * SLOTS, (128, 128)) == place
            request += lax.dot_general(left.astype(BF), right.astype(F32).astype(BF), (((1,), (1,)), ((), ())),
                                       preferred_element_type=F32)
    wanted = (request[:n_table] * 64.0 + request[n_table:]).astype(INT)
    for t in range(n_table):
        req[t] = wanted[t:t + 1, :]
    asked_ref[me_t] = req[me_t]

    @pl.loop(1, n_table)
    def _(i):
        peer = lax.rem(me_t + i, n_table)
        pltpu.make_async_remote_copy(
            src_ref=req.at[peer], dst_ref=asked_ref.at[me_t], send_sem=send_t.at[i], recv_sem=recv_t.at[me_t],
            device_id={"table": peer}, device_id_type=MESH).start()

    for copy in copies:
        copy.wait_send()

    @pl.loop(1, n_table)
    def _(i):
        peer = lax.rem(me_t + i, n_table)
        pltpu.make_async_remote_copy(
            src_ref=req.at[peer], dst_ref=asked_ref.at[peer], send_sem=send_t.at[i], recv_sem=recv_t.at[peer],
            device_id={"table": peer}, device_id_type=MESH).wait()


def route_call(n_dp, n_table, owners, rows, lengths, dest):
    seqs, events = rows.shape
    lines = events // 128
    vm = pl.BlockSpec(memory_space=pltpu.VMEM)
    sm = pl.BlockSpec(memory_space=pltpu.SMEM)
    return pl.pallas_call(
        functools.partial(route_kernel, seqs, n_dp, n_table),
        out_shape=(jax.ShapeDtypeStruct((n_table, 1, 128), INT), jax.ShapeDtypeStruct((seqs, lines, 128), INT)),
        in_specs=[vm, vm, sm, sm],
        out_specs=(vm, vm),
        scratch_shapes=[
            pltpu.VMEM((seqs * lines + 8, 128), INT),
            pltpu.VMEM((n_dp, seqs * lines + 8, 128), INT),
            pltpu.VMEM((n_table, 1, 128), INT),
            pltpu.SemaphoreType.DMA((n_dp,)),
            pltpu.SemaphoreType.DMA((n_dp,)),
            pltpu.SemaphoreType.DMA((n_table,)),
            pltpu.SemaphoreType.DMA((n_table,)),
        ],
        compiler_params=pltpu.CompilerParams(collective_id=0, has_side_effects=True),
        name="route",
    )(owners, rows, lengths, dest)


def on_device(owners, local_rows, lengths, destinations, table, gain_in, w_in, b_in, gain_out, w_out, b_out):
    seqs, events = local_rows.shape
    n_dp, n_table = lax.axis_size("dp"), lax.axis_size("table")
    asked, slot = route_call(n_dp, n_table, owners.reshape(seqs, events), local_rows, lengths, destinations)
    answers = []
    for s in range(seqs):
        wanted = asked[:, 0, s * SLOTS:(s + 1) * SLOTS].reshape(-1)
        found = jnp.take(table, wanted, axis=0, mode="clip").reshape(n_table, SLOTS, table.shape[1])
        answers.append(lax.all_to_all(found, "table", split_axis=0, concat_axis=0, tiled=True))
    out = None
    for s in range(seqs):
        out = layer_call(s, slot[s], answers[s].reshape(n_table * SLOTS, table.shape[1]),
                         gain_in, w_in, b_in, gain_out, w_out, b_out, out)
    return out


def solution(mesh):
    placed = (
        P(("dp", "table"), None, None),
        P(("dp", "table"), None),
        P(("dp", "table")),
        P("table", "dp"),
        P("table", None),
        P(),
        P(),
        P(),
        P(),
        P(),
        P(),
    )
    return jax.shard_map(
        on_device,
        mesh=mesh,
        in_specs=placed,
        out_specs=P(("dp", "table"), None, None),
        check_vma=False,
    )
```

time: 237 us -> 114 us (0.48)
  Pallas kernels: 0 us -> 62.7 us
  matrix products: 55.7 us -> 0 us
  local copies, waits for them, and re-layouts: 67.4 us -> 24.1 us
  blocking collectives: 29 us -> 0 us
  waiting for transfers between devices: 39.2 us -> 13.9 us
  other arithmetic: 25 us -> 0.02 us
  starting transfers between devices: 16.7 us -> 12.5 us
    pallas_call x0 -> x3, Pallas kernels: none -> 62.7 us  [the longest x2 39.2 us: layer_call(): pl.pallas_call(kernel, grid=(1,), in_specs=specs, out_specs=pl.BlockSpec(...]
    dot_general x8 -> x0, matrix products: 55.7 us -> none  [the longest x4 34.8 us: attend_block(): jnp.einsum('hqk,khd->qhd', weights, value_block, preferred_element_type=j...]
    all_to_all x3 -> x2, waiting for transfers between devices: 39.2 us -> 13.9 us  [on_device(): lax.all_to_all(found, 'table', split_axis=0, concat_axis=0, tiled=True)]
    all_to_all x1 -> x0, blocking collectives: 18.2 us -> none  [look_up(): lax.all_to_all(request, 'table', split_axis=0, concat_axis=0, tiled=True)]
    scatter x3 -> x0, local copies, waits for them, and re-layouts: 12.3 us -> none  [the longest x1 8.06 us: look_up(): jnp.zeros((shards * capacity,), jnp.int32).at[slot_index]]
    unnamed x1 -> x0, blocking collectives: 10.8 us -> none
    slice x13 -> x1, local copies, waits for them, and re-layouts: 11.2 us -> 0.91 us  [on_device(): wanted = asked[:, 0, s * SLOTS:(s + 1) * SLOTS].reshape(-1)]
    another operation x2 -> x0, other arithmetic: 9.27 us -> none
  transfers between devices with their start and end apart: 3 -> 2, of which waited for: 1 -> 1; matrix products, arithmetic and copies ran while one was open for 7% -> 7% of each run, Pallas kernels for 0% -> 17%
where the time goes in v1:
time: 114 us; the launch traced here: 113 us
  Pallas kernels  62.7 us (55%)
  local copies, waits for them, and re-layouts  24.1 us (21%)
  waiting for transfers between devices  13.9 us (12%)
  starting transfers between devices  12.5 us (11%)
    pallas_call x2, Pallas kernels, layer_call(): pl.pallas_call(kernel, grid=(1,), in_specs=specs, out_specs=pl.BlockSpec(...  39.2 us
    pallas_call x1, Pallas kernels, route_call(): pl.pallas_call(functools.partial(route_kernel, seqs, n_dp, n_table), out_...  23.5 us
    gather x2, local copies, waits for them, and re-layouts, on_device(): jnp.take(table, wanted, axis=0, mode='clip')  16.4 us
    all_to_all x2, waiting for transfers between devices, on_device(): lax.all_to_all(found, 'table', split_axis=0, concat_axis=0, tiled=True)  13.9 us
    all_to_all x2, starting transfers between devices, on_device(): lax.all_to_all(found, 'table', split_axis=0, concat_axis=0, tiled=True)  12.5 us
    unnamed x19, local copies, waits for them, and re-layouts  6.58 us
  transfers between devices with their start and end apart: 2, of which 1 were waited for; matrix products, arithmetic and copies ran while one was open for 7% of the time, Pallas kernels for 17%

profile of v1, /device:TPU:1, one launch (start us, length us, event | category | flops | bytes accessed | tf_op | source)
XLA Modules:
  0.0 113.2 jit_solution(16750493602007581256)
XLA Ops:
  0.0 1.3 %copy.15 = s32[2,1024,1]{1,0,2:T(2,128)} copy(s32[2,1024,1]{1,2,0:T(1,128)} %param.11) | data formatting | bytes 16384
  1.3 23.5 %route.1 = (s32[32,1,128]{2,1,0:T(1,128)}, s32[2,8,128]{2,1,0:T(8,128)}) custom-call(s32[2,1024]{1,0:T(2,128)} %bitcast.26, s32[2,1024]{1,0:T(2,128)} %rows_ref.1, s32[2]{0:T(128)} %lengths_ref.1, s32[1,2]{1,0:T(1,128)} %dest_ref.1), custom_call_target="tpu_custom_call" | custom-call | tf_op jit(solution)/shard_map/route/pallas_call | solution.py:240
  24.8 0.9 slice_reduce_fusion
  25.7 0.1 reshape.32
  25.8 8.2 %gather_fusion.1 = bf16[1536,512]{1,0:T(8,128)(2,1)} fusion(bf16[4096,512]{1,0:T(8,128)(2,1)} %param.15, s32[2048]{0:T(1024)S(1)} %pad_clamp_fusion), kind=kCustom, calls=%fused_computation.1 | custom fusion | bytes 3151872 | tf_op jit(solution)/shard_map/jit(_take)/gather | solution.py:266
  34.0 6.7 %all-to-all-start.1 = ((bf16[32,48,512]{2,1,0:T(8,128)(2,1)}), bf16[32,48,512]{2,1,0:T(8,128)(2,1)S(1)}, u32[]{:S(2)}, u32[]{:S(2)}) async-start(bf16[32,48,512]{2,1,0:T(8,128)(2,1)} %bitcast.8), calls=%async_computation.1 | async-start | bytes 3145728 | tf_op jit(solution)/shard_map/all_to_all | solution.py:267
  40.7 0.1 reshape.24
  40.8 8.2 %gather_fusion = bf16[1536,512]{1,0:T(8,128)(2,1)} fusion(bf16[4096,512]{1,0:T(8,128)(2,1)} %param.15, s32[2048]{0:T(1024)S(1)} %pad_clamp_fusion.1), kind=kCustom, calls=%fused_computation | custom fusion | bytes 3151872 | tf_op jit(solution)/shard_map/jit(_take)/gather | solution.py:266
  49.0 13.9 %all-to-all-done.1 = bf16[32,48,512]{2,1,0:T(8,128)(2,1)S(1)} async-done(((bf16[32,48,512]{2,1,0:T(8,128)(2,1)}), bf16[32,48,512]{2,1,0:T(8,128)(2,1)S(1)}, u32[]{:S(2)}, u32[]{:S(2)}) %all-to-all-start.1) | async-done | bytes 1572896 | tf_op jit(solution)/shard_map/all_to_all | solution.py:267
  62.9 0.0 copy-start.7
  62.9 5.8 %all-to-all-start = ((bf16[32,48,512]{2,1,0:T(8,128)(2,1)}), bf16[32,48,512]{2,1,0:T(8,128)(2,1)S(1)}, u32[]{:S(2)}, u32[]{:S(2)}) async-start(bf16[32,48,512]{2,1,0:T(8,128)(2,1)} %bitcast.25), calls=%async_computation | async-start | bytes 3145728 | tf_op jit(solution)/shard_map/all_to_all | solution.py:267
  68.7 0.0 copy-done.8
  68.7 0.0 copy-done.4
  68.7 0.0 copy-done.5
  68.7 0.0 copy-done.6
  68.7 0.0 copy-done.7
  68.7 0.0 copy-start
  68.7 1.6 %copy-done = bf16[512,2048]{1,0:T(8,128)(2,1)S(1)} copy-done((bf16[512,2048]{1,0:T(8,128)(2,1)S(1)}, bf16[512,2048]{1,0:T(8,128)(2,1)}, u32[]{:S(2)}) %copy-start) | copy-done | bytes 2097176
  70.3 1.0 copy-done.2
  71.4 19.7 %layer.2.refs_8_ = bf16[2,1024,512]{2,1,0:T(8,128)(2,1)} custom-call(s32[8,128]{1,0:T(8,128)S(1)} %get-tuple-element.11.slot_ref, bf16[1536,512]{1,0:T(8,128)(2,1)S(1)} %bitcast.15, f32[1,512]{1,0:T(1,128)S(1)} %bitcast.19, bf16[512,2048]{1,0:T(8,128)(2,1)S(1)} %copy-done, f32[1,2048]{1,0:T(1,128)S(1)} %bitcast.17, f32[1,512]{1,0:T(1,128)S(1)} %bitcast.21, ...), custom_call_target="tpu_custom_call" | custom-call | flops 8000000000 | bytes 8388608 | tf_op jit(solution)/shard_map/layer/pallas_call | solution.py:124
  91.0 0.0 all-to-all-done
  91.0 1.6 %copy-done.1 = bf16[512,2048]{1,0:T(8,128)(2,1)S(1)} copy-done((bf16[512,2048]{1,0:T(8,128)(2,1)S(1)}, bf16[512,2048]{1,0:T(8,128)(2,1)}, u32[]{:S(2)}) %copy-start.1) | copy-done | bytes 2097176
  92.6 1.0 copy-done.3
  93.7 19.6 %layer.3 = bf16[2,1024,512]{2,1,0:T(8,128)(2,1)} custom-call(s32[8,128]{1,0:T(8,128)S(1)} %get-tuple-element.12.refs_0_, bf16[1536,512]{1,0:T(8,128)(2,1)S(1)} %bitcast.16, f32[1,512]{1,0:T(1,128)S(1)} %bitcast.20, bf16[512,2048]{1,0:T(8,128)(2,1)S(1)} %copy-done.1, f32[1,2048]{1,0:T(1,128)S(1)} %bitcast.18, ...), custom_call_target="tpu_custom_call", output_to_operand_aliasing={{}: (8, {})} | custom-call | flops 8000000000 | bytes 8388608 | tf_op jit(solution)/shard_map/layer/pallas_call | solution.py:124
  (10 shorter events, 0.0 us)
Async XLA Ops:
  34.0 28.9 %all-to-all-start.1 = ((bf16[32,48,512]{2,1,0:T(8,128)(2,1)}), bf16[32,48,512]{2,1,0:T(8,128)(2,1)S(1)}, u32[]{:S(2)}, u32[]{:S(2)}) async-start(bf16[32,48,512]{2,1,0:T(8,128)(2,1)} %bitcast.8), calls=%async_computation.1 | async-start | bytes 3145728 | tf_op jit(solution)/shard_map/all_to_all | solution.py:267
  62.9 5.8 %copy-start.8 = (s32[2,8,128]{2,1,0:T(8,128)S(1)}, s32[2,8,128]{2,1,0:T(8,128)}, u32[]{:S(2)}) copy-start(s32[2,8,128]{2,1,0:T(8,128)} %get-tuple-element.7) | copy-start | bytes 24580
  62.9 5.8 %copy-start.4 = (f32[2048]{0:T(1024)S(1)}, f32[2048]{0:T(1024)}, u32[]{:S(2)}) copy-start(f32[2048]{0:T(1024)} %param.18) | copy-start | bytes 24580
  62.9 5.8 %copy-start.5 = (f32[512]{0:T(512)S(1)}, f32[512]{0:T(512)}, u32[]{:S(2)}) copy-start(f32[512]{0:T(512)} %param.16) | copy-start | bytes 6148
  62.9 5.8 %copy-start.6 = (f32[512]{0:T(512)S(1)}, f32[512]{0:T(512)}, u32[]{:S(2)}) copy-start(f32[512]{0:T(512)} %param.19) | copy-start | bytes 6148
  62.9 5.8 %copy-start.7 = (f32[512]{0:T(512)S(1)}, f32[512]{0:T(512)}, u32[]{:S(2)}) copy-start(f32[512]{0:T(512)} %param.21) | copy-start | bytes 6148
  62.9 28.1 %all-to-all-start = ((bf16[32,48,512]{2,1,0:T(8,128)(2,1)}), bf16[32,48,512]{2,1,0:T(8,128)(2,1)S(1)}, u32[]{:S(2)}, u32[]{:S(2)}) async-start(bf16[32,48,512]{2,1,0:T(8,128)(2,1)} %bitcast.25), calls=%async_computation | async-start | bytes 3145728 | tf_op jit(solution)/shard_map/all_to_all | solution.py:267
  68.7 1.6 %copy-start = (bf16[512,2048]{1,0:T(8,128)(2,1)S(1)}, bf16[512,2048]{1,0:T(8,128)(2,1)}, u32[]{:S(2)}) copy-start(bf16[512,2048]{1,0:T(8,128)(2,1)} %refs_3_.1) | copy-start | bytes 6291460
  70.3 1.0 copy-start.2
  91.0 1.6 %copy-start.1 = (bf16[512,2048]{1,0:T(8,128)(2,1)S(1)}, bf16[512,2048]{1,0:T(8,128)(2,1)}, u32[]{:S(2)}) copy-start(bf16[512,2048]{1,0:T(8,128)(2,1)} %refs_3_.1) | copy-start | bytes 6291460
  92.6 1.0 copy-start.3

commit v2 on v1

--- a/solution.py
+++ b/solution.py
@@ -146,8 +146,9 @@
 INT = jnp.int32
 
 
-def route_kernel(seqs, n_dp, n_table, owners_ref, rows_ref, lengths_ref, dest_ref, asked_ref, slot_ref,
-                 mine, every, req, send_z, recv_z, send_t, recv_t):
+def route_kernel(seqs, n_dp, n_table, owners_ref, rows_ref, lengths_ref, dest_ref, table_ref, slot_ref, answer_ref,
+                 mine, every, req, asked, wanted_rows, wide, picked, parcel, send_z, recv_z, send_t, recv_t, fetch_sem,
+                 send_rows, recv_rows):
     me_dp, me_t = lax.axis_index("dp"), lax.axis_index("table")
     events = owners_ref.shape[1]
     lines = events // 128
@@ -177,6 +178,11 @@
             device_id={"dp": lax.rem(me_dp + i, n_dp)}, device_id_type=MESH)
         copy.start()
         copies.append(copy)
+    @pl.loop(0, table_ref.shape[0] // 64)
+    def _(i):
+        at = pl.ds(pl.multiple_of(i * 64, 64), 64)
+        wide[at, :] = table_ref[at, :].astype(F32)
+
     for i in range(1, n_dp):
         pltpu.make_async_remote_copy(
             src_ref=mine, dst_ref=every.at[lax.rem(me_dp + i, n_dp)], send_sem=send_z.at[i],
@@ -212,13 +218,13 @@
     wanted = (request[:n_table] * 64.0 + request[n_table:]).astype(INT)
     for t in range(n_table):
         req[t] = wanted[t:t + 1, :]
-    asked_ref[me_t] = req[me_t]
+    asked[me_t] = req[me_t]
 
     @pl.loop(1, n_table)
     def _(i):
         peer = lax.rem(me_t + i, n_table)
         pltpu.make_async_remote_copy(
-            src_ref=req.at[peer], dst_ref=asked_ref.at[me_t], send_sem=send_t.at[i], recv_sem=recv_t.at[me_t],
+            src_ref=req.at[peer], dst_ref=asked.at[me_t], send_sem=send_t.at[i], recv_sem=recv_t.at[me_t],
             device_id={"table": peer}, device_id_type=MESH).start()
 
     for copy in copies:
@@ -228,43 +234,78 @@
     def _(i):
         peer = lax.rem(me_t + i, n_table)
         pltpu.make_async_remote_copy(
-            src_ref=req.at[peer], dst_ref=asked_ref.at[peer], send_sem=send_t.at[i], recv_sem=recv_t.at[peer],
+            src_ref=req.at[peer], dst_ref=asked.at[peer], send_sem=send_t.at[i], recv_sem=recv_t.at[peer],
             device_id={"table": peer}, device_id_type=MESH).wait()
 
-
-def route_call(n_dp, n_table, owners, rows, lengths, dest):
+    fetch = pltpu.make_async_copy(asked, wanted_rows, fetch_sem)
+    fetch.start()
+    fetch.wait()
+
+    def pick(s, peer):
+        for k in range(SLOTS):
+            picked[k:k + 1, :] = wide[pl.ds(wanted_rows[peer, 0, s * SLOTS + k] & (wide.shape[0] - 1), 1), :]
+
+    def row_copy(s, i, peer, other):
+        return pltpu.make_async_remote_copy(
+            src_ref=parcel.at[s, peer], dst_ref=answer_ref.at[s, other], send_sem=send_rows.at[s, i],
+            recv_sem=recv_rows.at[s, other], device_id={"table": peer}, device_id_type=MESH)
+
+    for s in range(seqs):
+        @pl.loop(1, n_table)
+        def _(i):
+            peer = lax.rem(me_t + i, n_table)
+            pick(s, peer)
+            parcel[s, peer] = picked[...].astype(BF)
+            row_copy(s, i, peer, me_t).start()
+
+        pick(s, me_t)
+        answer_ref[s, me_t] = picked[...].astype(BF)
+
+    for s in range(seqs):
+        @pl.loop(1, n_table)
+        def _(i):
+            peer = lax.rem(me_t + i, n_table)
+            row_copy(s, i, peer, peer).wait()
+
+
+def route_call(n_dp, n_table, owners, rows, lengths, dest, table):
     seqs, events = rows.shape
     lines = events // 128
     vm = pl.BlockSpec(memory_space=pltpu.VMEM)
     sm = pl.BlockSpec(memory_space=pltpu.SMEM)
     return pl.pallas_call(
         functools.partial(route_kernel, seqs, n_dp, n_table),
-        out_shape=(jax.ShapeDtypeStruct((n_table, 1, 128), INT), jax.ShapeDtypeStruct((seqs, lines, 128), INT)),
-        in_specs=[vm, vm, sm, sm],
+        out_shape=(jax.ShapeDtypeStruct((seqs, lines, 128), INT),
+                   jax.ShapeDtypeStruct((seqs, n_table, SLOTS, table.shape[1]), BF)),
+        in_specs=[vm, vm, sm, sm, vm],
         out_specs=(vm, vm),
         scratch_shapes=[
             pltpu.VMEM((seqs * lines + 8, 128), INT),
             pltpu.VMEM((n_dp, seqs * lines + 8, 128), INT),
             pltpu.VMEM((n_table, 1, 128), INT),
+            pltpu.VMEM((n_table, 1, 128), INT),
+            pltpu.SMEM((n_table, 1, 128), INT),
+            pltpu.VMEM(table.shape, F32),
+            pltpu.VMEM((SLOTS, table.shape[1]), F32),
+            pltpu.VMEM((seqs, n_table, SLOTS, table.shape[1]), BF),
             pltpu.SemaphoreType.DMA((n_dp,)),
             pltpu.SemaphoreType.DMA((n_dp,)),
             pltpu.SemaphoreType.DMA((n_table,)),
             pltpu.SemaphoreType.DMA((n_table,)),
+            pltpu.SemaphoreType.DMA,
+            pltpu.SemaphoreType.DMA((seqs, n_table)),
+            pltpu.SemaphoreType.DMA((seqs, n_table)),
         ],
-        compiler_params=pltpu.CompilerParams(collective_id=0, has_side_effects=True),
+        compiler_params=pltpu.CompilerParams(collective_id=0, has_side_effects=True, vmem_limit_bytes=40 << 20),
         name="route",
-    )(owners, rows, lengths, dest)
+    )(owners, rows, lengths, dest, table)
 
 
 def on_device(owners, local_rows, lengths, destinations, table, gain_in, w_in, b_in, gain_out, w_out, b_out):
     seqs, events = local_rows.shape
     n_dp, n_table = lax.axis_size("dp"), lax.axis_size("table")
-    asked, slot = route_call(n_dp, n_table, owners.reshape(seqs, events), local_rows, lengths, destinations)
-    answers = []
-    for s in range(seqs):
-        wanted = asked[:, 0, s * SLOTS:(s + 1) * SLOTS].reshape(-1)
-        found = jnp.take(table, wanted, axis=0, mode="clip").reshape(n_table, SLOTS, table.shape[1])
-        answers.append(lax.all_to_all(found, "table", split_axis=0, concat_axis=0, tiled=True))
+    slot, answers = route_call(
+        n_dp, n_table, owners.reshape(seqs, events), local_rows, lengths, destinations, table)
     out = None
     for s in range(seqs):
         out = layer_call(s, slot[s], answers[s].reshape(n_table * SLOTS, table.shape[1]),

time: 114 us -> 113 us (level)
  Pallas kernels: 62.7 us -> 106 us
  local copies, waits for them, and re-layouts: 24.1 us -> 6.53 us
  waiting for transfers between devices: 13.9 us -> 0 us
  starting transfers between devices: 12.5 us -> 0 us
    pallas_call x1, Pallas kernels: 23.5 us -> 66.4 us  [route_call(): pl.pallas_call(functools.partial(route_kernel, seqs, n_dp, n_table), out_...]
    gather x2 -> x0, local copies, waits for them, and re-layouts: 16.4 us -> none  [on_device(): jnp.take(table, wanted, axis=0, mode='clip')]
    all_to_all x2 -> x0, waiting for transfers between devices: 13.9 us -> none  [on_device(): lax.all_to_all(found, 'table', split_axis=0, concat_axis=0, tiled=True)]
    all_to_all x2 -> x0, starting transfers between devices: 12.5 us -> none  [on_device(): lax.all_to_all(found, 'table', split_axis=0, concat_axis=0, tiled=True)]
    unnamed x19 -> x21, local copies, waits for them, and re-layouts: 6.58 us -> 6.32 us
  transfers between devices with their start and end apart: 2 -> 0, of which waited for: 1 -> 0; matrix products, arithmetic and copies ran while one was open for 7% -> 0% of each run, Pallas kernels for 17% -> 0%
where the time goes in v2:
time: 113 us; the launch traced here: 112 us
  Pallas kernels  106 us (94%)
  local copies, waits for them, and re-layouts  6.53 us (6%)
    pallas_call x1, Pallas kernels, route_call(): pl.pallas_call(functools.partial(route_kernel, seqs, n_dp, n_table), out_...  66.4 us
    pallas_call x2, Pallas kernels, layer_call(): pl.pallas_call(kernel, grid=(1,), in_specs=specs, out_specs=pl.BlockSpec(...  39.3 us
    unnamed x21, local copies, waits for them, and re-layouts  6.32 us

profile of v2, /device:TPU:1, one launch (start us, length us, event | category | flops | bytes accessed | tf_op | source)
XLA Modules:
  0.0 112.4 jit_solution(4649948837161945630)
XLA Ops:
  0.0 0.7 copy.15
  0.7 0.0 copy-start
  0.7 2.2 %copy-done = bf16[4096,512]{1,0:T(8,128)(2,1)S(1)} copy-done((bf16[4096,512]{1,0:T(8,128)(2,1)S(1)}, bf16[4096,512]{1,0:T(8,128)(2,1)}, u32[]{:S(2)}) %copy-start) | copy-done | bytes 4194328
  2.9 0.0 copy-start.1
  2.9 0.7 copy-done.1
  3.6 0.0 copy-start.2
  3.6 0.7 copy-done.2
  4.2 0.7 copy-done.3
  4.9 66.4 %route.1 = (s32[2,8,128]{2,1,0:T(8,128)S(1)}, bf16[2,32,48,512]{3,2,1,0:T(8,128)(2,1)S(1)}) custom-call(s32[2,1024]{1,0:T(2,128)S(1)} %bitcast.15, s32[2,1024]{1,0:T(2,128)S(1)} %copy-done.1, s32[2]{0:T(128)S(1)} %copy-done.2, s32[1,2]{1,0:T(1,128)S(1)} %copy-done.3, bf16[4096,512]{1,0:T(8,128)(2,1)S(1)} %copy-done), custom_call_target="tpu_custom_call" | custom-call | tf_op jit(solution)/shard_map/route/pallas_call | solution.py:276
  71.4 0.0 copy-start.4
  71.4 0.0 copy-start.5
  71.4 0.0 copy-start.6
  71.4 0.0 copy-start.7
  71.4 0.0 copy-start.8
  71.4 0.0 copy-start.9
  71.4 0.2 fusion
  71.7 1.3 %copy-done.4 = bf16[512,2048]{1,0:T(8,128)(2,1)S(1)} copy-done((bf16[512,2048]{1,0:T(8,128)(2,1)S(1)}, bf16[512,2048]{1,0:T(8,128)(2,1)}, u32[]{:S(2)}) %copy-start.4) | copy-done | bytes 2097176
  73.0 0.1 copy-done.5
  73.0 0.0 copy-done.6
  73.0 0.0 copy-done.7
  73.0 0.0 copy-done.8
  73.1 0.0 copy-done.9
  73.1 19.7 %layer.2.refs_8_ = bf16[2,1024,512]{2,1,0:T(8,128)(2,1)} custom-call(s32[8,128]{1,0:T(8,128)S(1)} %get-tuple-element.11.slot_ref, bf16[1536,512]{1,0:T(8,128)(2,1)S(1)} %bitcast.14, f32[1,512]{1,0:T(1,128)S(1)} %bitcast.18, bf16[512,2048]{1,0:T(8,128)(2,1)S(1)} %copy-done.4, f32[1,2048]{1,0:T(1,128)S(1)} %bitcast.16, f32[1,512]{1,0:T(1,128)S(1)} %bitcast.20, ...), custom_call_target="tpu_custom_call" | custom-call | flops 8000000000 | bytes 8388608 | tf_op jit(solution)/shard_map/layer/pallas_call | solution.py:124
  92.7 19.6 %layer.3 = bf16[2,1024,512]{2,1,0:T(8,128)(2,1)} custom-call(s32[8,128]{1,0:T(8,128)S(1)} %get-tuple-element.12.refs_0_, bf16[1536,512]{1,0:T(8,128)(2,1)S(1)} %bitcast.13, f32[1,512]{1,0:T(1,128)S(1)} %bitcast.19, bf16[512,2048]{1,0:T(8,128)(2,1)S(1)} %copy-done.4, f32[1,2048]{1,0:T(1,128)S(1)} %bitcast.17, ...), custom_call_target="tpu_custom_call", output_to_operand_aliasing={{}: (8, {})} | custom-call | flops 8000000000 | bytes 8388608 | tf_op jit(solution)/shard_map/layer/pallas_call | solution.py:124
  (2 shorter events, 0.0 us)
Async XLA Ops:
  0.7 2.2 %copy-start = (bf16[4096,512]{1,0:T(8,128)(2,1)S(1)}, bf16[4096,512]{1,0:T(8,128)(2,1)}, u32[]{:S(2)}) copy-start(bf16[4096,512]{1,0:T(8,128)(2,1)} %table_ref.1) | copy-start | bytes 12582916
  2.9 0.7 copy-start.1
  3.6 0.7 copy-start.2
  4.2 0.7 copy-start.3
  71.4 1.6 %copy-start.4 = (bf16[512,2048]{1,0:T(8,128)(2,1)S(1)}, bf16[512,2048]{1,0:T(8,128)(2,1)}, u32[]{:S(2)}) copy-start(bf16[512,2048]{1,0:T(8,128)(2,1)} %refs_3_.1) | copy-start | bytes 6291460
  71.4 1.7 %copy-start.5 = (bf16[512,512]{1,0:T(8,128)(2,1)S(1)}, bf16[512,512]{1,0:T(8,128)(2,1)}, u32[]{:S(2)}) copy-start(bf16[512,512]{1,0:T(8,128)(2,1)} %refs_6_.1) | copy-start | bytes 1572868
  71.4 1.7 %copy-start.6 = (f32[2048]{0:T(1024)S(1)}, f32[2048]{0:T(1024)}, u32[]{:S(2)}) copy-start(f32[2048]{0:T(1024)} %param.18) | copy-start | bytes 24580
  71.4 1.6 %copy-start.7 = (f32[512]{0:T(512)S(1)}, f32[512]{0:T(512)}, u32[]{:S(2)}) copy-start(f32[512]{0:T(512)} %param.16) | copy-start | bytes 6148
  71.4 1.6 %copy-start.8 = (f32[512]{0:T(512)S(1)}, f32[512]{0:T(512)}, u32[]{:S(2)}) copy-start(f32[512]{0:T(512)} %param.19) | copy-start | bytes 6148
  71.4 1.6 %copy-start.9 = (f32[512]{0:T(512)S(1)}, f32[512]{0:T(512)}, u32[]{:S(2)}) copy-start(f32[512]{0:T(512)} %param.21) | copy-start | bytes 6148

commit v3 on v2

--- a/solution.py
+++ b/solution.py
@@ -11,6 +11,9 @@
 BLK = 256
 BF = jnp.bfloat16
 F32 = jnp.float32
+INT = jnp.int32
+MESH = pl.DeviceIdType.MESH
+SLOTS = 48
 
 
 def silu_half(u):
@@ -24,8 +27,8 @@
     return spread * lax.rsqrt(variance + EPS) * gain
 
 
-def layer_kernel(slot_ref, rows_ref, gain_in_ref, w_in_ref, b_in_ref, gain_out_ref, w_out_ref, b_out_ref,
-                 out_ref, hist, gate, q, k, v0, v1, att):
+def layer_body(slot_ref, rows_ref, weights, out_ref, done, hist, gate, q, k, v0, v1, att):
+    gain_in_ref, w_in_ref, b_in_ref, gain_out_ref, w_out_ref, b_out_ref = weights
     events, width = hist.shape
     slots = rows_ref.shape[0]
     lanes = lax.broadcasted_iota(jnp.int32, (128, 128), 1)
@@ -100,58 +103,46 @@
         full = jnp.concatenate([att[p, at, :] for p in range(4)], axis=1)
         gated = (norm_rows(full, gain_out_ref[...]) * gate[at, :]).astype(BF)
         update = jnp.dot(gated, w_out_ref[...], preferred_element_type=F32) + b_out_ref[...]
-        out_ref[0, at, :] = jnp.where(here, hist[at, :].astype(F32) + update, 0.0).astype(BF)
+        out_ref[at, :] = jnp.where(here, hist[at, :].astype(F32) + update, 0.0).astype(BF)
+        done(c, at)
         return carry
 
     lax.fori_loop(0, events // BLK, finish, 0)
 
 
-def layer_call(s, slot, rows, gain_in, w_in, b_in, gain_out, w_out, b_out, before):
-    events = slot.shape[0] * 128
-    width = rows.shape[1]
-    vm = pl.BlockSpec(memory_space=pltpu.VMEM)
-    ins = [slot, rows, gain_in[None], w_in, b_in[None], gain_out[None], w_out, b_out[None]]
-    specs = [vm] * len(ins)
-    kernel = layer_kernel
-    aliases = {}
-    if before is not None:
-        ins.append(before)
-        specs.append(pl.BlockSpec(memory_space=pl.ANY))
-        aliases = {len(ins) - 1: 0}
-
-        def kernel(*refs):
-            layer_kernel(*refs[:8], *refs[9:])
-    return pl.pallas_call(
-        kernel,
-        grid=(1,),
-        in_specs=specs,
-        out_specs=pl.BlockSpec((1, events, width), lambda i: (s, 0, 0)),
-        out_shape=jax.ShapeDtypeStruct((2, events, width), BF),
-        scratch_shapes=[
-            pltpu.VMEM((events, width), BF),
-            pltpu.VMEM((events, width), F32),
-            pltpu.VMEM((4, events, 128), BF),
-            pltpu.VMEM((4, events, 128), BF),
-            pltpu.VMEM((4, events, 128), BF),
-            pltpu.VMEM((4, events, 128), BF),
-            pltpu.VMEM((4, events, 128), F32),
-        ],
-        input_output_aliases=aliases,
-        compiler_params=pltpu.CompilerParams(vmem_limit_bytes=40 << 20),
-        cost_estimate=pl.CostEstimate(flops=8 * 10**9, bytes_accessed=8 << 20, transcendentals=8 << 20),
-        name="layer",
-    )(*ins)
-MESH = pl.DeviceIdType.MESH
-SLOTS = 48
-INT = jnp.int32
-
-
-def route_kernel(seqs, n_dp, n_table, owners_ref, rows_ref, lengths_ref, dest_ref, table_ref, slot_ref, answer_ref,
-                 mine, every, req, asked, wanted_rows, wide, picked, parcel, send_z, recv_z, send_t, recv_t, fetch_sem,
-                 send_rows, recv_rows):
+def layer_scratch(events):
+    return [
+        pltpu.VMEM((events, 512), BF),
+        pltpu.VMEM((events, 512), F32),
+        pltpu.VMEM((4, events, 128), BF),
+        pltpu.VMEM((4, events, 128), BF),
+        pltpu.VMEM((4, events, 128), BF),
+        pltpu.VMEM((4, events, 128), BF),
+        pltpu.VMEM((4, events, 128), F32),
+    ]
+
+
+def weight_scratch(weights):
+    return [pltpu.VMEM(w.shape, w.dtype) for w in weights] + [pltpu.SemaphoreType.DMA((len(weights),))]
+
+
+def fetch_kernel(seqs, n_dp, n_table, owners_hbm, rows_hbm, lengths_hbm, dest_hbm, table_hbm, *refs):
+    weights_hbm, refs = refs[:6], refs[6:]
+    slot_ref, later_ref, out_ref = refs[:3]
+    (owners, rows, lengths, dest, table, local_sem), refs = refs[3:9], refs[9:]
+    weights, weight_sem, refs = refs[:6], refs[6], refs[7:]
+    (mine, every, req, asked, wanted_rows, wide, picked, parcel, first,
+     send_z, recv_z, send_t, recv_t, fetch_sem, send_rows, recv_rows), work = refs[:16], refs[16:]
     me_dp, me_t = lax.axis_index("dp"), lax.axis_index("table")
-    events = owners_ref.shape[1]
+    events = rows.shape[1]
     lines = events // 128
+
+    inputs = [(owners_hbm, owners), (rows_hbm, rows), (lengths_hbm, lengths), (dest_hbm, dest), (table_hbm, table)]
+    local = [pltpu.make_async_copy(a, b, local_sem.at[i]) for i, (a, b) in enumerate(inputs)]
+    local += [pltpu.make_async_copy(a, b, weight_sem.at[i]) for i, (a, b) in enumerate(zip(weights_hbm, weights))]
+    for copy in local:
+        copy.start()
+
     barrier = pltpu.get_barrier_semaphore()
     for i in range(1, n_dp):
         pl.semaphore_signal(barrier, inc=1, device_id={"dp": lax.rem(me_dp + i, n_dp)}, device_id_type=MESH)
@@ -160,14 +151,16 @@
     def _(i):
         pl.semaphore_signal(barrier, inc=1, device_id={"table": lax.rem(me_t + i, n_table)}, device_id_type=MESH)
 
+    for copy in local[:4]:
+        copy.wait()
     lane = lax.broadcasted_iota(INT, (1, 128), 1)
     for s in range(seqs):
         for r in range(lines):
             cs = slice(r * 128, (r + 1) * 128)
-            packed = owners_ref[s:s + 1, cs] * 4096 + rows_ref[s:s + 1, cs]
-            mine[s * lines + r:s * lines + r + 1, :] = jnp.where(lane + r * 128 < lengths_ref[s], packed, -1)
+            packed = owners[s, :, cs] * 4096 + rows[s:s + 1, cs]
+            mine[s * lines + r:s * lines + r + 1, :] = jnp.where(lane + r * 128 < lengths[s], packed, -1)
     for j in range(8):
-        mine[seqs * lines + j:seqs * lines + j + 1, :] = jnp.zeros((1, 128), INT) + dest_ref[0, min(j, seqs - 1)]
+        mine[seqs * lines + j:seqs * lines + j + 1, :] = jnp.zeros((1, 128), INT) + dest[0, min(j, seqs - 1)]
     every[me_dp] = mine[...]
     pl.semaphore_wait(barrier, n_dp - 1 + n_table - 1)
 
@@ -178,11 +171,15 @@
             device_id={"dp": lax.rem(me_dp + i, n_dp)}, device_id_type=MESH)
         copy.start()
         copies.append(copy)
-    @pl.loop(0, table_ref.shape[0] // 64)
-    def _(i):
-        at = pl.ds(pl.multiple_of(i * 64, 64), 64)
-        wide[at, :] = table_ref[at, :].astype(F32)
-
+    def widen(begin, end):
+        @pl.loop(begin, end)
+        def _(i):
+            at = pl.ds(pl.multiple_of(i * 64, 64), 64)
+            wide[at, :] = table[at, :].astype(F32)
+
+    chunks = table.shape[0] // 64
+    local[4].wait()
+    widen(0, chunks // 2)
     for i in range(1, n_dp):
         pltpu.make_async_remote_copy(
             src_ref=mine, dst_ref=every.at[lax.rem(me_dp + i, n_dp)], send_sem=send_z.at[i],
@@ -227,6 +224,7 @@
             src_ref=req.at[peer], dst_ref=asked.at[me_t], send_sem=send_t.at[i], recv_sem=recv_t.at[me_t],
             device_id={"table": peer}, device_id_type=MESH).start()
 
+    widen(chunks // 2, chunks)
     for copy in copies:
         copy.wait_send()
 
@@ -241,13 +239,17 @@
     fetch.start()
     fetch.wait()
 
+    def part(t):
+        return pl.ds(pl.multiple_of(t * SLOTS, SLOTS), SLOTS)
+
     def pick(s, peer):
         for k in range(SLOTS):
-            picked[k:k + 1, :] = wide[pl.ds(wanted_rows[peer, 0, s * SLOTS + k] & (wide.shape[0] - 1), 1), :]
+            row = wanted_rows[peer, 0, s * SLOTS + k] & (wide.shape[0] - 1)
+            picked[k:k + 1, :] = wide[pl.ds(row, 1), :]
 
     def row_copy(s, i, peer, other):
         return pltpu.make_async_remote_copy(
-            src_ref=parcel.at[s, peer], dst_ref=answer_ref.at[s, other], send_sem=send_rows.at[s, i],
+            src_ref=parcel.at[s, peer], dst_ref=(first, later_ref)[s].at[part(other)], send_sem=send_rows.at[s, i],
             recv_sem=recv_rows.at[s, other], device_id={"table": peer}, device_id_type=MESH)
 
     for s in range(seqs):
@@ -259,35 +261,51 @@
             row_copy(s, i, peer, me_t).start()
 
         pick(s, me_t)
-        answer_ref[s, me_t] = picked[...].astype(BF)
-
-    for s in range(seqs):
+        (first, later_ref)[s][part(me_t), :] = picked[...].astype(BF)
+
+    for copy in local[5:]:
+        copy.wait()
+
+    def settle(s):
         @pl.loop(1, n_table)
         def _(i):
             peer = lax.rem(me_t + i, n_table)
             row_copy(s, i, peer, peer).wait()
 
-
-def route_call(n_dp, n_table, owners, rows, lengths, dest, table):
+    settle(0)
+    layer_body(slot_ref.at[0], first, weights, out_ref, lambda c, at: None, *work)
+    settle(1)
+
+
+def fetch_call(n_dp, n_table, owners, rows, lengths, dest, table, weights):
     seqs, events = rows.shape
-    lines = events // 128
+    lines, width = events // 128, table.shape[1]
+    any_space = pl.BlockSpec(memory_space=pl.ANY)
     vm = pl.BlockSpec(memory_space=pltpu.VMEM)
-    sm = pl.BlockSpec(memory_space=pltpu.SMEM)
     return pl.pallas_call(
-        functools.partial(route_kernel, seqs, n_dp, n_table),
+        functools.partial(fetch_kernel, seqs, n_dp, n_table),
         out_shape=(jax.ShapeDtypeStruct((seqs, lines, 128), INT),
-                   jax.ShapeDtypeStruct((seqs, n_table, SLOTS, table.shape[1]), BF)),
-        in_specs=[vm, vm, sm, sm, vm],
-        out_specs=(vm, vm),
+                   jax.ShapeDtypeStruct((n_table * SLOTS, width), BF),
+                   jax.ShapeDtypeStruct((events, width), BF)),
+        in_specs=[any_space] * (5 + len(weights)),
+        out_specs=(vm, vm, vm),
         scratch_shapes=[
+            pltpu.VMEM(owners.shape, INT),
+            pltpu.VMEM(rows.shape, INT),
+            pltpu.SMEM(lengths.shape, INT),
+            pltpu.SMEM(dest.shape, INT),
+            pltpu.VMEM(table.shape, BF),
+            pltpu.SemaphoreType.DMA((5,)),
+            *weight_scratch(weights),
             pltpu.VMEM((seqs * lines + 8, 128), INT),
             pltpu.VMEM((n_dp, seqs * lines + 8, 128), INT),
             pltpu.VMEM((n_table, 1, 128), INT),
             pltpu.VMEM((n_table, 1, 128), INT),
             pltpu.SMEM((n_table, 1, 128), INT),
             pltpu.VMEM(table.shape, F32),
-            pltpu.VMEM((SLOTS, table.shape[1]), F32),
-            pltpu.VMEM((seqs, n_table, SLOTS, table.shape[1]), BF),
+            pltpu.VMEM((SLOTS, width), F32),
+            pltpu.VMEM((seqs, n_table, SLOTS, width), BF),
+            pltpu.VMEM((n_table * SLOTS, width), BF),
             pltpu.SemaphoreType.DMA((n_dp,)),
             pltpu.SemaphoreType.DMA((n_dp,)),
             pltpu.SemaphoreType.DMA((n_table,)),
@@ -295,22 +313,63 @@
             pltpu.SemaphoreType.DMA,
             pltpu.SemaphoreType.DMA((seqs, n_table)),
             pltpu.SemaphoreType.DMA((seqs, n_table)),
+            *layer_scratch(events),
         ],
-        compiler_params=pltpu.CompilerParams(collective_id=0, has_side_effects=True, vmem_limit_bytes=40 << 20),
-        name="route",
-    )(owners, rows, lengths, dest, table)
+        compiler_params=pltpu.CompilerParams(collective_id=0, has_side_effects=True, vmem_limit_bytes=60 << 20),
+        name="fetch",
+    )(owners, rows, lengths, dest, table, *weights)
+
+
+def last_kernel(slot_ref, rows_ref, ready_ref, *refs):
+    weights_hbm, out_hbm, refs = refs[:6], refs[6], refs[7:]
+    weights, weight_sem, refs = refs[:6], refs[6], refs[7:]
+    out, ready_sem, out_sem, work = refs[0], refs[1], refs[2], refs[3:]
+    local = [pltpu.make_async_copy(a, b, weight_sem.at[i]) for i, (a, b) in enumerate(zip(weights_hbm, weights))]
+    for copy in local:
+        copy.start()
+    ready = pltpu.make_async_copy(ready_ref, out_hbm.at[0], ready_sem)
+    ready.start()
+    for copy in local:
+        copy.wait()
+
+    def send(c, at):
+        pltpu.make_async_copy(out.at[at], out_hbm.at[1, at], out_sem.at[c]).start()
+
+    layer_body(slot_ref.at[1], rows_ref, weights, out, send, *work)
+    for c in range(out.shape[0] // BLK):
+        at = pl.ds(c * BLK, BLK)
+        pltpu.make_async_copy(out.at[at], out_hbm.at[1, at], out_sem.at[c]).wait()
+    ready.wait()
+
+
+def last_call(slot, rows, ready, weights):
+    events, width = ready.shape
+    any_space = pl.BlockSpec(memory_space=pl.ANY)
+    vm = pl.BlockSpec(memory_space=pltpu.VMEM)
+    return pl.pallas_call(
+        last_kernel,
+        out_shape=jax.ShapeDtypeStruct((2, events, width), BF),
+        in_specs=[vm, vm, vm] + [any_space] * len(weights),
+        out_specs=any_space,
+        scratch_shapes=[
+            *weight_scratch(weights),
+            pltpu.VMEM((events, width), BF),
+            pltpu.SemaphoreType.DMA,
+            pltpu.SemaphoreType.DMA((events // BLK,)),
+            *layer_scratch(events),
+        ],
+        compiler_params=pltpu.CompilerParams(vmem_limit_bytes=60 << 20),
+        name="last",
+    )(slot, rows, ready, *weights)
 
 
 def on_device(owners, local_rows, lengths, destinations, table, gain_in, w_in, b_in, gain_out, w_out, b_out):
     seqs, events = local_rows.shape
     n_dp, n_table = lax.axis_size("dp"), lax.axis_size("table")
-    slot, answers = route_call(
-        n_dp, n_table, owners.reshape(seqs, events), local_rows, lengths, destinations, table)
-    out = None
-    for s in range(seqs):
-        out = layer_call(s, slot[s], answers[s].reshape(n_table * SLOTS, table.shape[1]),
-                         gain_in, w_in, b_in, gain_out, w_out, b_out, out)
-    return out
+    weights = (gain_in[None], w_in, b_in[None], gain_out[None], w_out, b_out[None])
+    slot, rows, ready = fetch_call(
+        n_dp, n_table, owners.reshape(seqs, 1, events), local_rows, lengths, destinations, table, weights)
+    return last_call(slot, rows, ready, weights)
 
 
 def solution(mesh):

time: 113 us -> 95.2 us (0.84)
  Pallas kernels: 106 us -> 95.1 us
  local copies, waits for them, and re-layouts: 6.53 us -> 0 us
    pallas_call x3 -> x2, Pallas kernels: 106 us -> 95.1 us  [the longest x1 71.7 us: fetch_call(): pl.pallas_call(functools.partial(fetch_kernel, seqs, n_dp, n_table), out_...]
    unnamed x21 -> x0, local copies, waits for them, and re-layouts: 6.32 us -> none
where the time goes in v3:
time: 95.2 us; the launch traced here: 95.1 us
  Pallas kernels  95.1 us (100%)
    pallas_call x1, Pallas kernels, fetch_call(): pl.pallas_call(functools.partial(fetch_kernel, seqs, n_dp, n_table), out_...  71.7 us
    pallas_call x1, Pallas kernels, last_call(): pl.pallas_call(last_kernel, out_shape=jax.ShapeDtypeStruct((2, events, wi...  23.4 us

profile of v3, /device:TPU:1, one launch (start us, length us, event | category | flops | bytes accessed | tf_op | source)
XLA Modules:
  0.0 95.1 jit_solution(11911604221727277524)
XLA Ops:
  0.0 71.7 %fetch.1 = (s32[2,8,128]{2,1,0:T(8,128)}, bf16[1536,512]{1,0:T(8,128)(2,1)}, bf16[1024,512]{1,0:T(8,128)(2,1)}) custom-call(s32[2,1,1024]{2,1,0:T(1,128)} %bitcast.7, s32[2,1024]{1,0:T(2,128)} %rows_hbm.1, s32[2]{0:T(128)} %lengths_hbm.1, s32[1,2]{1,0:T(1,128)} %dest_hbm.1, bf16[4096,512]{1,0:T(8,128)(2,1)} %table_hbm.1, f32[1,512]{1,0:T(1,128)} %bitcast.8, ...), custom_call_target="tpu_custom_call" | custom-call | tf_op jit(solution)/shard_map/fetch/pallas_call | solution.py:285
  71.7 23.4 %last.1 = bf16[2,1024,512]{2,1,0:T(8,128)(2,1)} custom-call(s32[2,8,128]{2,1,0:T(8,128)} %get-tuple-element.8.slot_ref, bf16[1536,512]{1,0:T(8,128)(2,1)} %get-tuple-element.9.rows_ref, bf16[1024,512]{1,0:T(8,128)(2,1)} %get-tuple-element.10.ready_ref, f32[1,512]{1,0:T(1,128)} %bitcast.9, bf16[512,2048]{1,0:T(8,128)(2,1)} %refs_1_.3, f32[1,2048]{1,0:T(1,128)} %bitcast.6, ...), custom_call_target="tpu_custom_call" | custom-call | tf_op jit(solution)/shard_map/last/pallas_call | solution.py:349

commit v4 on v3

--- a/solution.py
+++ b/solution.py
@@ -132,7 +132,8 @@
     (owners, rows, lengths, dest, table, local_sem), refs = refs[3:9], refs[9:]
     weights, weight_sem, refs = refs[:6], refs[6], refs[7:]
     (mine, every, req, asked, wanted_rows, wide, picked, parcel, first,
-     send_z, recv_z, send_t, recv_t, fetch_sem, send_rows, recv_rows), work = refs[:16], refs[16:]
+     send_z, recv_z, send_t, recv_t, fetch_sem, send_rows, recv_rows,
+     relay, relay_in, relay_out), work = refs[:19], refs[19:]
     me_dp, me_t = lax.axis_index("dp"), lax.axis_index("table")
     events = rows.shape[1]
     lines = events // 128
@@ -247,34 +248,116 @@
             row = wanted_rows[peer, 0, s * SLOTS + k] & (wide.shape[0] - 1)
             picked[k:k + 1, :] = wide[pl.ds(row, 1), :]
 
-    def row_copy(s, i, peer, other):
+    y0, x0, c0 = me_t // 8, me_t // 2 % 4, me_t % 2
+
+    def at_offset(dy, dx, dc):
+        return (y0 + dy) % 4 * 8 + (x0 + dx) % 4 * 2 + (c0 + dc) % 2
+
+    def detour(j):
+        late = j // 4
+        dy = (1 - late) * 2 + late * ((j + 4) % 4 + j // 6)
+        dx = (1 - late) * (j % 4) + late * 2
+        return dy, dx, dy // 2 * (3 - dy) * 3, dx // 2 * (3 - dx) * 3
+
+    def straight(k):
+        late = k // 15
+        m = (k + 9) % 24 % 9
+        dy = (1 - late) * ((k + 1) // 4) + late * (m // 3 + m // 6)
+        dx = (1 - late) * ((k + 1) % 4) + late * (m % 3 + m % 3 // 2)
+        return dy, dx, late
+
+    landing = (first, later_ref)
+
+    def send_straight(s, k):
+        dy, dx, dc = straight(k)
+        peer = at_offset(dy, dx, dc)
+        return peer, pltpu.make_async_remote_copy(
+            src_ref=parcel.at[s, peer], dst_ref=landing[s].at[part(me_t)], send_sem=send_rows.at[s, peer],
+            recv_sem=recv_rows.at[s, me_t], device_id={"table": peer}, device_id_type=MESH)
+
+    def send_halfway(s, j):
+        dy, dx, hy, hx = detour(j)
+        peer = at_offset(dy, dx, 1)
+        return peer, pltpu.make_async_remote_copy(
+            src_ref=parcel.at[s, peer], dst_ref=relay.at[s, j], send_sem=send_rows.at[s, peer],
+            recv_sem=relay_in.at[s, j], device_id={"table": at_offset(hy, hx, 0)}, device_id_type=MESH)
+
+    def send_on(s, j):
+        dy, dx, hy, hx = detour(j)
+        origin = at_offset(4 - hy, 4 - hx, 0)
         return pltpu.make_async_remote_copy(
-            src_ref=parcel.at[s, peer], dst_ref=(first, later_ref)[s].at[part(other)], send_sem=send_rows.at[s, i],
-            recv_sem=recv_rows.at[s, other], device_id={"table": peer}, device_id_type=MESH)
-
+            src_ref=relay.at[s, j], dst_ref=landing[s].at[part(origin)], send_sem=relay_out.at[s, j],
+            recv_sem=recv_rows.at[s, origin], device_id={"table": at_offset(4 + dy - hy, 4 + dx - hx, 1)},
+            device_id_type=MESH)
+
+    def load(s, peer):
+        pick(s, peer)
+        parcel[s, peer] = picked[...].astype(BF)
+
+    def all_halfway(s):
+        @pl.loop(0, 7)
+        def _(j):
+            peer, copy = send_halfway(s, j)
+            load(s, peer)
+            copy.start()
+
+    def all_straight(s):
+        @pl.loop(0, 24)
+        def _(k):
+            peer, copy = send_straight(s, k)
+            load(s, peer)
+            copy.start()
+
+    def all_on(s):
+        @pl.loop(0, 7)
+        def _(j):
+            send_halfway(s, j)[1].wait_recv()
+            send_on(s, j).start()
+
+    all_halfway(0)
+    all_straight(0)
+    all_halfway(1)
+    all_on(0)
+    all_straight(1)
     for s in range(seqs):
-        @pl.loop(1, n_table)
-        def _(i):
-            peer = lax.rem(me_t + i, n_table)
-            pick(s, peer)
-            parcel[s, peer] = picked[...].astype(BF)
-            row_copy(s, i, peer, me_t).start()
-
         pick(s, me_t)
-        (first, later_ref)[s][part(me_t), :] = picked[...].astype(BF)
-
+        landing[s][part(me_t), :] = picked[...].astype(BF)
+    all_on(1)
     for copy in local[5:]:
         copy.wait()
 
     def settle(s):
-        @pl.loop(1, n_table)
-        def _(i):
-            peer = lax.rem(me_t + i, n_table)
-            row_copy(s, i, peer, peer).wait()
+        @pl.loop(0, 24)
+        def _(k):
+            dy, dx, dc = straight(k)
+            source = at_offset(4 - dy, 4 - dx, dc)
+            pltpu.make_async_remote_copy(
+                src_ref=parcel.at[s, source], dst_ref=landing[s].at[part(source)], send_sem=send_rows.at[s, source],
+                recv_sem=recv_rows.at[s, source], device_id={"table": source}, device_id_type=MESH).wait_recv()
+
+        @pl.loop(0, 7)
+        def _(j):
+            dy, dx, hy, hx = detour(j)
+            source = at_offset(4 - dy, 4 - dx, 1)
+            pltpu.make_async_remote_copy(
+                src_ref=parcel.at[s, source], dst_ref=landing[s].at[part(source)], send_sem=send_rows.at[s, source],
+                recv_sem=recv_rows.at[s, source], device_id={"table": source}, device_id_type=MESH).wait_recv()
+
+    def sent(s):
+        @pl.loop(0, 24)
+        def _(k):
+            send_straight(s, k)[1].wait_send()
+
+        @pl.loop(0, 7)
+        def _(j):
+            send_halfway(s, j)[1].wait_send()
+            send_on(s, j).wait_send()
 
     settle(0)
     layer_body(slot_ref.at[0], first, weights, out_ref, lambda c, at: None, *work)
     settle(1)
+    sent(0)
+    sent(1)
 
 
 def fetch_call(n_dp, n_table, owners, rows, lengths, dest, table, weights):
@@ -313,6 +396,9 @@
             pltpu.SemaphoreType.DMA,
             pltpu.SemaphoreType.DMA((seqs, n_table)),
             pltpu.SemaphoreType.DMA((seqs, n_table)),
+            pltpu.VMEM((seqs, 7, SLOTS, width), BF),
+            pltpu.SemaphoreType.DMA((seqs, 7)),
+            pltpu.SemaphoreType.DMA((seqs, 7)),
             *layer_scratch(events),
         ],
         compiler_params=pltpu.CompilerParams(collective_id=0, has_side_effects=True, vmem_limit_bytes=60 << 20),

time: 95.2 us -> 109 us (1.14)
  Pallas kernels: 95.1 us -> 109 us
    pallas_call x1, Pallas kernels: 71.7 us -> 85.2 us  [fetch_call(): pl.pallas_call(functools.partial(fetch_kernel, seqs, n_dp, n_table), out_...]
where the time goes in v4:
time: 109 us
  Pallas kernels  109 us (100%)
    pallas_call x1, Pallas kernels, fetch_call(): pl.pallas_call(functools.partial(fetch_kernel, seqs, n_dp, n_table), out_...  85.2 us
    pallas_call x1, Pallas kernels, last_call(): pl.pallas_call(last_kernel, out_shape=jax.ShapeDtypeStruct((2, events, wi...  23.4 us

profile of v4, /device:TPU:1, one launch (start us, length us, event | category | flops | bytes accessed | tf_op | source)
XLA Modules:
  0.0 108.6 jit_solution(14740328761760161396)
XLA Ops:
  0.0 85.2 %fetch.1 = (s32[2,8,128]{2,1,0:T(8,128)}, bf16[1536,512]{1,0:T(8,128)(2,1)}, bf16[1024,512]{1,0:T(8,128)(2,1)}) custom-call(s32[2,1,1024]{2,1,0:T(1,128)} %bitcast.7, s32[2,1024]{1,0:T(2,128)} %rows_hbm.1, s32[2]{0:T(128)} %lengths_hbm.1, s32[1,2]{1,0:T(1,128)} %dest_hbm.1, bf16[4096,512]{1,0:T(8,128)(2,1)} %table_hbm.1, f32[1,512]{1,0:T(1,128)} %bitcast.8, ...), custom_call_target="tpu_custom_call" | custom-call | tf_op jit(solution)/shard_map/fetch/pallas_call | solution.py:368
  85.2 23.4 %last.1 = bf16[2,1024,512]{2,1,0:T(8,128)(2,1)} custom-call(s32[2,8,128]{2,1,0:T(8,128)} %get-tuple-element.8.slot_ref, bf16[1536,512]{1,0:T(8,128)(2,1)} %get-tuple-element.9.rows_ref, bf16[1024,512]{1,0:T(8,128)(2,1)} %get-tuple-element.10.ready_ref, f32[1,512]{1,0:T(1,128)} %bitcast.9, bf16[512,2048]{1,0:T(8,128)(2,1)} %refs_1_.3, f32[1,2048]{1,0:T(1,128)} %bitcast.6, ...), custom_call_target="tpu_custom_call" | custom-call | tf_op jit(solution)/shard_map/last/pallas_call | solution.py:435

commit v5 on v3

--- a/solution.py
+++ b/solution.py
@@ -48,11 +48,11 @@
         rows = jnp.dot(pick, rows_ref[...], preferred_element_type=F32)
         at = pl.ds(pl.multiple_of(c * BLK, BLK), BLK)
         hist[at, :] = rows.astype(BF)
-        normed = norm_rows(rows, gain_in_ref[...]).astype(BF)
+        normed = norm_rows(rows, gain_in_ref[...] * 0.5).astype(BF)
         for part in range(4):
             cs = slice(part * width, (part + 1) * width)
-            pre = jnp.dot(normed, w_in_ref[:, cs], preferred_element_type=F32) + b_in_ref[:, cs]
-            act = silu_half(0.5 * pre)
+            pre = jnp.dot(normed, w_in_ref[:, cs], preferred_element_type=F32) + b_in_ref[:, cs] * 0.5
+            act = silu_half(pre)
             if part == 0:
                 gate[at, :] = act
             elif part == 1:
@@ -62,32 +62,34 @@
                     v0[p, at, :] = jnp.where(half, piece, 0.0).astype(BF)
                     v1[p, at, :] = jnp.where(half, 0.0, piece).astype(BF)
             else:
-                target = q if part == 2 else k
-                act = act.astype(BF)
                 for p in range(4):
-                    target[p, at, :] = act[:, p * 128:(p + 1) * 128]
+                    piece = act[:, p * 128:(p + 1) * 128]
+                    if part == 3:
+                        k[p, at, :] = piece.astype(BF)
+                    else:
+                        piece = piece * 0.0625
+                        q[2 * p, at, :] = jnp.where(half, piece, 0.0).astype(BF)
+                        q[2 * p + 1, at, :] = jnp.where(half, 0.0, piece).astype(BF)
         return carry
 
-    lax.fori_loop(0, events // BLK, project, 0)
+    lax.fori_loop(0, events // BLK, project, 0, unroll=True)
 
     tri = lax.broadcasted_iota(jnp.int32, (BLK, BLK), 0) >= lax.broadcasted_iota(jnp.int32, (BLK, BLK), 1)
 
     def attend(p, carry):
-        for i in range(events // BLK):
-            at = slice(i * BLK, (i + 1) * BLK)
-            qb = q[p, at, :] * jnp.bfloat16(0.0625)
-            total = None
+        for j in range(events // BLK):
+            ks = slice(j * BLK, (j + 1) * BLK)
+            rest = slice(j * BLK, events)
             for h, v in ((0, v0), (1, v1)):
-                qh = jnp.where(half == (h == 0), qb.astype(F32), 0.0).astype(BF)
-                for j in range(i + 1):
-                    ks = slice(j * BLK, (j + 1) * BLK)
-                    s = lax.dot_general(qh, k[p, ks, :], (((1,), (1,)), ((), ())), preferred_element_type=F32)
-                    w = silu_half(s)
-                    if j == i:
-                        w = jnp.where(tri, w, 0.0)
-                    o = jnp.dot(w.astype(BF), v[p, ks, :], preferred_element_type=F32)
-                    total = o if total is None else total + o
-            att[p, at, :] = total
+                s = lax.dot_general(q[2 * p + h, rest, :], k[p, ks, :], (((1,), (1,)), ((), ())), preferred_element_type=F32)
+                w = silu_half(s)
+                head = jnp.where(tri, w[:BLK], 0.0).astype(BF)
+                w = jnp.concatenate([head, w[BLK:].astype(BF)], axis=0) if j < events // BLK - 1 else head
+                o = jnp.dot(w, v[p, ks, :], preferred_element_type=F32)
+                if j == 0 and h == 0:
+                    att[p, rest, :] = o
+                else:
+                    att[p, rest, :] += o
         return carry
 
     lax.fori_loop(0, 4, attend, 0)
@@ -107,14 +109,14 @@
         done(c, at)
         return carry
 
-    lax.fori_loop(0, events // BLK, finish, 0)
+    lax.fori_loop(0, events // BLK, finish, 0, unroll=True)
 
 
 def layer_scratch(events):
     return [
         pltpu.VMEM((events, 512), BF),
         pltpu.VMEM((events, 512), F32),
-        pltpu.VMEM((4, events, 128), BF),
+        pltpu.VMEM((8, events, 128), BF),
         pltpu.VMEM((4, events, 128), BF),
         pltpu.VMEM((4, events, 128), BF),
         pltpu.VMEM((4, events, 128), BF),
@@ -252,13 +254,17 @@
             src_ref=parcel.at[s, peer], dst_ref=(first, later_ref)[s].at[part(other)], send_sem=send_rows.at[s, i],
             recv_sem=recv_rows.at[s, other], device_id={"table": peer}, device_id_type=MESH)
 
+    turn = lax.rem(me_t * 7, n_table - 1)
+    y0, x0, c0 = me_t // 8, me_t // 2 % 4, me_t % 2
+
     for s in range(seqs):
-        @pl.loop(1, n_table)
-        def _(i):
-            peer = lax.rem(me_t + i, n_table)
+        @pl.loop(0, n_table - 1)
+        def _(k):
+            i = lax.rem(k + turn, n_table - 1) + 1
+            peer = (y0 + i // 8) % 4 * 8 + (x0 + i // 2 % 4) % 4 * 2 + (c0 + i % 2) % 2
             pick(s, peer)
             parcel[s, peer] = picked[...].astype(BF)
-            row_copy(s, i, peer, me_t).start()
+            row_copy(s, peer, peer, me_t).start()
 
         pick(s, me_t)
         (first, later_ref)[s][part(me_t), :] = picked[...].astype(BF)
@@ -270,7 +276,7 @@
         @pl.loop(1, n_table)
         def _(i):
             peer = lax.rem(me_t + i, n_table)
-            row_copy(s, i, peer, peer).wait()
+            row_copy(s, peer, peer, peer).wait()
 
     settle(0)
     layer_body(slot_ref.at[0], first, weights, out_ref, lambda c, at: None, *work)

time: 95.2 us -> 89.6 us (0.941)
  Pallas kernels: 95.1 us -> 89.3 us
    pallas_call x1, Pallas kernels: 23.4 us -> 18.9 us  [last_call(): pl.pallas_call(last_kernel, out_shape=jax.ShapeDtypeStruct((2, events, wi...]
    pallas_call x1, Pallas kernels: 71.7 us -> 70.4 us  [fetch_call(): pl.pallas_call(functools.partial(fetch_kernel, seqs, n_dp, n_table), out_...]
where the time goes in v5:
time: 89.6 us; the launch traced here: 89.5 us
  Pallas kernels  89.3 us (100%)
    pallas_call x1, Pallas kernels, fetch_call(): pl.pallas_call(functools.partial(fetch_kernel, seqs, n_dp, n_table), out_...  70.4 us
    pallas_call x1, Pallas kernels, last_call(): pl.pallas_call(last_kernel, out_shape=jax.ShapeDtypeStruct((2, events, wi...  18.9 us

profile of v5, /device:TPU:1, one launch (start us, length us, event | category | flops | bytes accessed | tf_op | source)
XLA Modules:
  0.0 89.5 jit_solution(13459661084726700128)
XLA Ops:
  0.0 70.4 %fetch.1 = (s32[2,8,128]{2,1,0:T(8,128)}, bf16[1536,512]{1,0:T(8,128)(2,1)}, bf16[1024,512]{1,0:T(8,128)(2,1)}) custom-call(s32[2,1,1024]{2,1,0:T(1,128)} %bitcast.7, s32[2,1024]{1,0:T(2,128)} %rows_hbm.1, s32[2]{0:T(128)} %lengths_hbm.1, s32[1,2]{1,0:T(1,128)} %dest_hbm.1, bf16[4096,512]{1,0:T(8,128)(2,1)} %table_hbm.1, f32[1,512]{1,0:T(1,128)} %bitcast.8, ...), custom_call_target="tpu_custom_call" | custom-call | tf_op jit(solution)/shard_map/fetch/pallas_call | solution.py:291
  70.5 18.9 %last.1 = bf16[2,1024,512]{2,1,0:T(8,128)(2,1)} custom-call(s32[2,8,128]{2,1,0:T(8,128)} %get-tuple-element.8.slot_ref, bf16[1536,512]{1,0:T(8,128)(2,1)} %get-tuple-element.9.rows_ref, bf16[1024,512]{1,0:T(8,128)(2,1)} %get-tuple-element.10.ready_ref, f32[1,512]{1,0:T(1,128)} %bitcast.9, bf16[512,2048]{1,0:T(8,128)(2,1)} %refs_1_.3, f32[1,2048]{1,0:T(1,128)} %bitcast.6, ...), custom_call_target="tpu_custom_call" | custom-call | tf_op jit(solution)/shard_map/last/pallas_call | solution.py:355

commit v6 on v5

--- a/solution.py
+++ b/solution.py
@@ -27,7 +27,7 @@
     return spread * lax.rsqrt(variance + EPS) * gain
 
 
-def layer_body(slot_ref, rows_ref, weights, out_ref, done, hist, gate, q, k, v0, v1, att):
+def layer_body(slot_ref, rows_ref, weights, out_ref, done, hist, gate, q, k, v, att):
     gain_in_ref, w_in_ref, b_in_ref, gain_out_ref, w_out_ref, b_out_ref = weights
     events, width = hist.shape
     slots = rows_ref.shape[0]
@@ -59,8 +59,8 @@
                 act = act * here
                 for p in range(4):
                     piece = act[:, p * 128:(p + 1) * 128]
-                    v0[p, at, :] = jnp.where(half, piece, 0.0).astype(BF)
-                    v1[p, at, :] = jnp.where(half, 0.0, piece).astype(BF)
+                    v[p, c, :BLK, :] = jnp.where(half, piece, 0.0).astype(BF)
+                    v[p, c, BLK:, :] = jnp.where(half, 0.0, piece).astype(BF)
             else:
                 for p in range(4):
                     piece = act[:, p * 128:(p + 1) * 128]
@@ -80,16 +80,17 @@
         for j in range(events // BLK):
             ks = slice(j * BLK, (j + 1) * BLK)
             rest = slice(j * BLK, events)
-            for h, v in ((0, v0), (1, v1)):
+            both = []
+            for h in range(2):
                 s = lax.dot_general(q[2 * p + h, rest, :], k[p, ks, :], (((1,), (1,)), ((), ())), preferred_element_type=F32)
                 w = silu_half(s)
                 head = jnp.where(tri, w[:BLK], 0.0).astype(BF)
-                w = jnp.concatenate([head, w[BLK:].astype(BF)], axis=0) if j < events // BLK - 1 else head
-                o = jnp.dot(w, v[p, ks, :], preferred_element_type=F32)
-                if j == 0 and h == 0:
-                    att[p, rest, :] = o
-                else:
-                    att[p, rest, :] += o
+                both.append(jnp.concatenate([head, w[BLK:].astype(BF)], axis=0) if j < events // BLK - 1 else head)
+            o = jnp.dot(jnp.concatenate(both, axis=1), v[p, j], preferred_element_type=F32)
+            if j == 0:
+                att[p, rest, :] = o
+            else:
+                att[p, rest, :] += o
         return carry
 
     lax.fori_loop(0, 4, attend, 0)
@@ -118,8 +119,7 @@
         pltpu.VMEM((events, 512), F32),
         pltpu.VMEM((8, events, 128), BF),
         pltpu.VMEM((4, events, 128), BF),
-        pltpu.VMEM((4, events, 128), BF),
-        pltpu.VMEM((4, events, 128), BF),
+        pltpu.VMEM((4, events // BLK, 2 * BLK, 128), BF),
         pltpu.VMEM((4, events, 128), F32),
     ]
 
@@ -130,11 +130,11 @@
 
 def fetch_kernel(seqs, n_dp, n_table, owners_hbm, rows_hbm, lengths_hbm, dest_hbm, table_hbm, *refs):
     weights_hbm, refs = refs[:6], refs[6:]
-    slot_ref, later_ref, out_ref = refs[:3]
-    (owners, rows, lengths, dest, table, local_sem), refs = refs[3:9], refs[9:]
+    out_hbm = refs[0]
+    (owners, rows, lengths, dest, table, local_sem), refs = refs[1:7], refs[7:]
     weights, weight_sem, refs = refs[:6], refs[6], refs[7:]
-    (mine, every, req, asked, wanted_rows, wide, picked, parcel, first,
-     send_z, recv_z, send_t, recv_t, fetch_sem, send_rows, recv_rows), work = refs[:16], refs[16:]
+    (mine, every, req, asked, wanted_rows, wide, picked, parcel, landing, slot_ref, out,
+     send_z, recv_z, send_t, recv_t, fetch_sem, send_rows, recv_rows, out_sem), work = refs[:19], refs[19:]
     me_dp, me_t = lax.axis_index("dp"), lax.axis_index("table")
     events = rows.shape[1]
     lines = events // 128
@@ -251,7 +251,7 @@
 
     def row_copy(s, i, peer, other):
         return pltpu.make_async_remote_copy(
-            src_ref=parcel.at[s, peer], dst_ref=(first, later_ref)[s].at[part(other)], send_sem=send_rows.at[s, i],
+            src_ref=parcel.at[s, peer], dst_ref=landing.at[s, part(other)], send_sem=send_rows.at[s, i],
             recv_sem=recv_rows.at[s, other], device_id={"table": peer}, device_id_type=MESH)
 
     turn = lax.rem(me_t * 7, n_table - 1)
@@ -267,7 +267,7 @@
             row_copy(s, peer, peer, me_t).start()
 
         pick(s, me_t)
-        (first, later_ref)[s][part(me_t), :] = picked[...].astype(BF)
+        landing[s, part(me_t), :] = picked[...].astype(BF)
 
     for copy in local[5:]:
         copy.wait()
@@ -278,23 +278,29 @@
             peer = lax.rem(me_t + i, n_table)
             row_copy(s, peer, peer, peer).wait()
 
-    settle(0)
-    layer_body(slot_ref.at[0], first, weights, out_ref, lambda c, at: None, *work)
-    settle(1)
+    def leave(s, c):
+        at = pl.ds(c * BLK, BLK)
+        return pltpu.make_async_copy(out.at[s, at], out_hbm.at[s, at], out_sem.at[s, c])
+
+    @pl.loop(0, seqs)
+    def _(s):
+        settle(s)
+        layer_body(slot_ref.at[s], landing.at[s], weights, out.at[s], lambda c, at: leave(s, c).start(), *work)
+
+    for s in range(seqs):
+        for c in range(events // BLK):
+            leave(s, c).wait()
 
 
 def fetch_call(n_dp, n_table, owners, rows, lengths, dest, table, weights):
     seqs, events = rows.shape
     lines, width = events // 128, table.shape[1]
     any_space = pl.BlockSpec(memory_space=pl.ANY)
-    vm = pl.BlockSpec(memory_space=pltpu.VMEM)
     return pl.pallas_call(
         functools.partial(fetch_kernel, seqs, n_dp, n_table),
-        out_shape=(jax.ShapeDtypeStruct((seqs, lines, 128), INT),
-                   jax.ShapeDtypeStruct((n_table * SLOTS, width), BF),
-                   jax.ShapeDtypeStruct((events, width), BF)),
+        out_shape=jax.ShapeDtypeStruct((seqs, events, width), BF),
         in_specs=[any_space] * (5 + len(weights)),
-        out_specs=(vm, vm, vm),
+        out_specs=any_space,
         scratch_shapes=[
             pltpu.VMEM(owners.shape, INT),
             pltpu.VMEM(rows.shape, INT),
@@ -311,7 +317,9 @@
             pltpu.VMEM(table.shape, F32),
             pltpu.VMEM((SLOTS, width), F32),
             pltpu.VMEM((seqs, n_table, SLOTS, width), BF),
-            pltpu.VMEM((n_table * SLOTS, width), BF),
+            pltpu.VMEM((seqs, n_table * SLOTS, width), BF),
+            pltpu.VMEM((seqs, lines, 128), INT),
+            pltpu.VMEM((seqs, events, width), BF),
             pltpu.SemaphoreType.DMA((n_dp,)),
             pltpu.SemaphoreType.DMA((n_dp,)),
             pltpu.SemaphoreType.DMA((n_table,)),
@@ -319,6 +327,7 @@
             pltpu.SemaphoreType.DMA,
             pltpu.SemaphoreType.DMA((seqs, n_table)),
             pltpu.SemaphoreType.DMA((seqs, n_table)),
+            pltpu.SemaphoreType.DMA((seqs, events // BLK)),
             *layer_scratch(events),
         ],
         compiler_params=pltpu.CompilerParams(collective_id=0, has_side_effects=True, vmem_limit_bytes=60 << 20),
@@ -326,56 +335,12 @@
     )(owners, rows, lengths, dest, table, *weights)
 
 
-def last_kernel(slot_ref, rows_ref, ready_ref, *refs):
-    weights_hbm, out_hbm, refs = refs[:6], refs[6], refs[7:]
-    weights, weight_sem, refs = refs[:6], refs[6], refs[7:]
-    out, ready_sem, out_sem, work = refs[0], refs[1], refs[2], refs[3:]
-    local = [pltpu.make_async_copy(a, b, weight_sem.at[i]) for i, (a, b) in enumerate(zip(weights_hbm, weights))]
-    for copy in local:
-        copy.start()
-    ready = pltpu.make_async_copy(ready_ref, out_hbm.at[0], ready_sem)
-    ready.start()
-    for copy in local:
-        copy.wait()
-
-    def send(c, at):
-        pltpu.make_async_copy(out.at[at], out_hbm.at[1, at], out_sem.at[c]).start()
-
-    layer_body(slot_ref.at[1], rows_ref, weights, out, send, *work)
-    for c in range(out.shape[0] // BLK):
-        at = pl.ds(c * BLK, BLK)
-        pltpu.make_async_copy(out.at[at], out_hbm.at[1, at], out_sem.at[c]).wait()
-    ready.wait()
-
-
-def last_call(slot, rows, ready, weights):
-    events, width = ready.shape
-    any_space = pl.BlockSpec(memory_space=pl.ANY)
-    vm = pl.BlockSpec(memory_space=pltpu.VMEM)
-    return pl.pallas_call(
-        last_kernel,
-        out_shape=jax.ShapeDtypeStruct((2, events, width), BF),
-        in_specs=[vm, vm, vm] + [any_space] * len(weights),
-        out_specs=any_space,
-        scratch_shapes=[
-            *weight_scratch(weights),
-            pltpu.VMEM((events, width), BF),
-            pltpu.SemaphoreType.DMA,
-            pltpu.SemaphoreType.DMA((events // BLK,)),
-            *layer_scratch(events),
-        ],
-        compiler_params=pltpu.CompilerParams(vmem_limit_bytes=60 << 20),
-        name="last",
-    )(slot, rows, ready, *weights)
-
-
 def on_device(owners, local_rows, lengths, destinations, table, gain_in, w_in, b_in, gain_out, w_out, b_out):
     seqs, events = local_rows.shape
     n_dp, n_table = lax.axis_size("dp"), lax.axis_size("table")
     weights = (gain_in[None], w_in, b_in[None], gain_out[None], w_out, b_out[None])
-    slot, rows, ready = fetch_call(
+    return fetch_call(
         n_dp, n_table, owners.reshape(seqs, 1, events), local_rows, lengths, destinations, table, weights)
-    return last_call(slot, rows, ready, weights)
 
 
 def solution(mesh):

time: 89.6 us -> 86.6 us (0.967)
  Pallas kernels: 89.3 us -> 83.5 us
  local copies, waits for them, and re-layouts: 0 us -> 3.05 us
    pallas_call x1 -> x0, Pallas kernels: 18.9 us -> none  [last_call(): pl.pallas_call(last_kernel, out_shape=jax.ShapeDtypeStruct((2, events, wi...]
    pallas_call x1, Pallas kernels: 70.4 us -> 83.5 us  [fetch_call(): pl.pallas_call(functools.partial(fetch_kernel, seqs, n_dp, n_table), out_...]
    unnamed x0 -> x1, local copies, waits for them, and re-layouts: none -> 3.05 us
where the time goes in v6:
time: 86.6 us; the launch traced here: 86.5 us
  Pallas kernels  83.5 us (96%)
  local copies, waits for them, and re-layouts  3.05 us (4%)
    pallas_call x1, Pallas kernels, fetch_call(): pl.pallas_call(functools.partial(fetch_kernel, seqs, n_dp, n_table), out_...  83.5 us
    unnamed x1, local copies, waits for them, and re-layouts  3.05 us

profile of v6, /device:TPU:1, one launch (start us, length us, event | category | flops | bytes accessed | tf_op | source)
XLA Modules:
  0.0 86.5 jit_solution(12797979019706408579)
XLA Ops:
  0.0 83.5 %fetch.1 = bf16[2,1024,512]{2,1,0:T(8,128)(2,1)} custom-call(s32[2,1,1024]{2,1,0:T(1,128)} %bitcast.5, s32[2,1024]{1,0:T(2,128)} %rows_hbm.1, s32[2]{0:T(128)} %lengths_hbm.1, s32[1,2]{1,0:T(1,128)} %dest_hbm.1, bf16[4096,512]{1,0:T(8,128)(2,1)} %table_hbm.1, f32[1,512]{1,0:T(1,128)} %bitcast.7, bf16[512,2048]{1,0:T(8,128)(2,1)} %refs_1_.1, ...), custom_call_target="tpu_custom_call" | custom-call | tf_op jit(solution)/shard_map/fetch/pallas_call | solution.py:299
  83.5 3.0 %copy.13 = bf16[2,1024,512]{2,1,0:T(8,128)(2,1)} copy(bf16[2,1024,512]{2,1,0:T(8,128)(2,1)} %fetch.1) | data formatting | bytes 4194304

commit v7 on v6

--- a/solution.py
+++ b/solution.py
@@ -254,13 +254,13 @@
             src_ref=parcel.at[s, peer], dst_ref=landing.at[s, part(other)], send_sem=send_rows.at[s, i],
             recv_sem=recv_rows.at[s, other], device_id={"table": peer}, device_id_type=MESH)
 
-    turn = lax.rem(me_t * 7, n_table - 1)
+    turn = lax.rem(me_t * 11, n_table - 1)
     y0, x0, c0 = me_t // 8, me_t // 2 % 4, me_t % 2
 
     for s in range(seqs):
         @pl.loop(0, n_table - 1)
         def _(k):
-            i = lax.rem(k + turn, n_table - 1) + 1
+            i = lax.rem(k * 3 + turn, n_table - 1) + 1
             peer = (y0 + i // 8) % 4 * 8 + (x0 + i // 2 % 4) % 4 * 2 + (c0 + i % 2) % 2
             pick(s, peer)
             parcel[s, peer] = picked[...].astype(BF)

time: 86.6 us -> 81.7 us (0.943)
  the two profiles are of different devices: /device:TPU:1 before, /device:TPU:7 now
where the time goes in v7:
time: 81.7 us; the launch traced here: 81.6 us
  Pallas kernels  78.6 us (96%)
  local copies, waits for them, and re-layouts  3.05 us (4%)
    pallas_call x1, Pallas kernels, fetch_call(): pl.pallas_call(functools.partial(fetch_kernel, seqs, n_dp, n_table), out_...  78.6 us
    unnamed x1, local copies, waits for them, and re-layouts  3.05 us

profile of v7, /device:TPU:7, one launch (start us, length us, event | category | flops | bytes accessed | tf_op | source)
XLA Modules:
  0.0 81.6 jit_solution(11612873830973235427)
XLA Ops:
  0.0 78.6 %fetch.1 = bf16[2,1024,512]{2,1,0:T(8,128)(2,1)} custom-call(s32[2,1,1024]{2,1,0:T(1,128)} %bitcast.5, s32[2,1024]{1,0:T(2,128)} %rows_hbm.1, s32[2]{0:T(128)} %lengths_hbm.1, s32[1,2]{1,0:T(1,128)} %dest_hbm.1, bf16[4096,512]{1,0:T(8,128)(2,1)} %table_hbm.1, f32[1,512]{1,0:T(1,128)} %bitcast.7, bf16[512,2048]{1,0:T(8,128)(2,1)} %refs_1_.1, ...), custom_call_target="tpu_custom_call" | custom-call | tf_op jit(solution)/shard_map/fetch/pallas_call | solution.py:299
  78.6 3.0 %copy.13 = bf16[2,1024,512]{2,1,0:T(8,128)(2,1)} copy(bf16[2,1024,512]{2,1,0:T(8,128)(2,1)} %fetch.1) | data formatting | bytes 4194304

commit v8 on v7

--- a/solution.py
+++ b/solution.py
@@ -260,7 +260,7 @@
     for s in range(seqs):
         @pl.loop(0, n_table - 1)
         def _(k):
-            i = lax.rem(k * 3 + turn, n_table - 1) + 1
+            i = lax.rem(k * 5 + turn, n_table - 1) + 1
             peer = (y0 + i // 8) % 4 * 8 + (x0 + i // 2 % 4) % 4 * 2 + (c0 + i % 2) % 2
             pick(s, peer)
             parcel[s, peer] = picked[...].astype(BF)

time: 81.7 us -> 80.5 us (0.985)
  the two profiles are of different devices: /device:TPU:7 before, /device:TPU:1 now
where the time goes in v8:
time: 80.5 us; the launch traced here: 80.4 us
  Pallas kernels  77.4 us (96%)
  local copies, waits for them, and re-layouts  3.05 us (4%)
    pallas_call x1, Pallas kernels, fetch_call(): pl.pallas_call(functools.partial(fetch_kernel, seqs, n_dp, n_table), out_...  77.4 us
    unnamed x1, local copies, waits for them, and re-layouts  3.05 us

profile of v8, /device:TPU:1, one launch (start us, length us, event | category | flops | bytes accessed | tf_op | source)
XLA Modules:
  0.0 80.4 jit_solution(2824540941127582079)
XLA Ops:
  0.0 77.4 %fetch.1 = bf16[2,1024,512]{2,1,0:T(8,128)(2,1)} custom-call(s32[2,1,1024]{2,1,0:T(1,128)} %bitcast.5, s32[2,1024]{1,0:T(2,128)} %rows_hbm.1, s32[2]{0:T(128)} %lengths_hbm.1, s32[1,2]{1,0:T(1,128)} %dest_hbm.1, bf16[4096,512]{1,0:T(8,128)(2,1)} %table_hbm.1, f32[1,512]{1,0:T(1,128)} %bitcast.7, bf16[512,2048]{1,0:T(8,128)(2,1)} %refs_1_.1, ...), custom_call_target="tpu_custom_call" | custom-call | tf_op jit(solution)/shard_map/fetch/pallas_call | solution.py:299
  77.4 3.0 %copy.13 = bf16[2,1024,512]{2,1,0:T(8,128)(2,1)} copy(bf16[2,1024,512]{2,1,0:T(8,128)(2,1)} %fetch.1) | data formatting | bytes 4194304
